TPU v7x, 32 devices: a whole 2x2x4 slice. The times are simulated.
32 devices in a mesh: groups: 2 (over x), expert: 16 (over z, y, core).
Axes of the slice: x: 2, y: 2, z: 4, core: 2. Of those that a mesh axis runs over, the one named last changes fastest.
Arguments:
- tokens: bfloat16 [2048, 4096], P(('groups', 'expert')), parts along dimension 0, may hold values from -6 to 6
- routes: int32 [2048, 8], P(('groups', 'expert')), parts along dimension 0, may hold values from 0 to 7, as said below
- route_weights: float32 [2048, 8], P(('groups', 'expert')), parts along dimension 0, may hold values from 0.05 to 0.25
- slot_experts: int32 [8], replicated, may hold values from 0 to 7, each once
- gateup_base: bfloat16 [16, 4096, 768], P('expert'), may hold values from -0.09375 to 0.09375
- down_base: bfloat16 [16, 384, 4096], P('expert'), may hold values from -0.21875 to 0.21875
- entry_factor: bfloat16 [8, 4096, 64], P(None, 'expert'), may hold values from -0.09375 to 0.09375
- gating_factor: bfloat16 [8, 1536, 64], P(None, 'expert'), may hold values from -0.75 to 0.75
- hidden_factor: bfloat16 [8, 768, 64], P(None, 'expert'), may hold values from -0.21875 to 0.21875
- output_factor: bfloat16 [8, 4096, 64], P(None, 'expert'), may hold values from -0.75 to 0.75
Outputs:
- mixed: bfloat16 [2048, 4096], P(('groups', 'expert')), parts along dimension 0
There are 2 independent parts, one for each index of `groups`. A program takes and returns all parts, laid end to end along the dimension named above; an argument that names none is the same for every part. Nothing has to cross between parts.
Inputs may be any that keep to these rules, and one draw needn't show every extreme that they name: `routes`: each row names 8 different experts. Within the rows of one device (aligned blocks of 64 rows) each expert is named at least 64 and at most 64 times, and in every draw one expert is named exactly 64 times within the rows of every device.
All inputs are finite; a program needn't handle non-finite values.
Results may differ from a plain program's by a relative error of at most 0.0062.
Values may be sent and summed in bfloat16 or wider, within the bound.
No kernel may reach another device: no remote copies, remote signals or barrier semaphores. Data moves between devices by JAX's collectives and lax.ppermute only.
A program may use at most 128 MiB of HBM per device.

v0:
```python
import jax
import jax.numpy as jnp
from jax import lax
from jax.sharding import PartitionSpec as P

adapter_scale = 0.5


def partner(block, axis, apart):
    count = lax.axis_size(axis)
    route = []
    for low in range(count):
        high = low | 1 << apart
        if high != low and high < count:
            route += [(low, high), (high, low)]
    return lax.ppermute(block, axis, route)


def contracted_rows(left, right):
    return lax.dot_general(
        left, right, (((1,), (1,)), ((), ())), preferred_element_type=jnp.float32
    )


def expert_block(
    row_block,
    near_gateup,
    far_gateup,
    near_down,
    far_down,
    entry_rows,
    gating_rows,
    hidden_rows,
    output_matrix_rows,
    parity,
):
    width_half = near_gateup.shape[1] // 2
    hidden_width = hidden_rows.shape[0]
    local_start = parity * width_half
    remote_start = (1 - parity) * width_half
    local_product = jnp.dot(row_block, near_gateup, preferred_element_type=jnp.float32)
    remote_product = jnp.dot(row_block, far_gateup, preferred_element_type=jnp.float32)
    rank_rows = jnp.dot(row_block, entry_rows, preferred_element_type=jnp.float32).astype(
        jnp.bfloat16
    )
    adapter_gateup = contracted_rows(rank_rows, gating_rows)

    def column_tile_block(begin):
        return lax.dynamic_slice_in_dim(adapter_gateup, begin, width_half, 1)

    local_gate = local_product[:, :width_half] + adapter_scale * column_tile_block(local_start)
    local_up = local_product[:, width_half:] + adapter_scale * column_tile_block(
        hidden_width + local_start
    )
    remote_gate = remote_product[:, :width_half] + adapter_scale * column_tile_block(remote_start)
    remote_up = remote_product[:, width_half:] + adapter_scale * column_tile_block(
        hidden_width + remote_start
    )
    hidden_near = (jax.nn.silu(local_gate) * local_up).astype(jnp.bfloat16)
    hidden_far = (jax.nn.silu(remote_gate) * remote_up).astype(jnp.bfloat16)
    base_result_rows = jnp.dot(hidden_near, near_down, preferred_element_type=jnp.float32)
    base_result_rows = base_result_rows + jnp.dot(
        hidden_far, far_down, preferred_element_type=jnp.float32
    )
    rank_near = lax.dynamic_slice_in_dim(hidden_rows, local_start, width_half, 0)
    rank_far = lax.dynamic_slice_in_dim(hidden_rows, remote_start, width_half, 0)
    adapter_rank = jnp.dot(hidden_near, rank_near, preferred_element_type=jnp.float32)
    adapter_rank = (
        adapter_rank + jnp.dot(hidden_far, rank_far, preferred_element_type=jnp.float32)
    ).astype(jnp.bfloat16)
    return (
        base_result_rows + adapter_scale * contracted_rows(adapter_rank, output_matrix_rows)
    ).astype(jnp.bfloat16)


def unpack_factors(received, model_width, hidden_width):
    devices = received.shape[0]
    width_rows = model_width // devices
    hidden_rows = hidden_width // devices
    entry_rows = received[:, :width_rows].reshape(model_width, -1)
    output_matrix_rows = received[:, width_rows : 2 * width_rows].reshape(model_width, -1)
    gating_rows = received[:, 2 * width_rows : 2 * width_rows + 2 * hidden_rows].reshape(
        2 * hidden_width, -1
    )
    down_rows = received[:, 2 * width_rows + 2 * hidden_rows :].reshape(hidden_width, -1)
    return (entry_rows, gating_rows, down_rows, output_matrix_rows)


def per_device(
    tokens,
    routes,
    route_weights,
    slot_experts,
    gateup_base,
    down_base,
    entry_factor,
    gating_factor,
    hidden_factor,
    output_factor,
):
    devices = lax.axis_size("expert")
    experts = devices // 2
    tok_dev, top_count = routes.shape
    model_width = tokens.shape[1]
    hidden_width = hidden_factor.shape[1] * devices
    mean_load = tok_dev * top_count // experts
    capacity = min(mean_load + 2, tok_dev)
    half_cap = capacity // 2
    stacked = jnp.concatenate((entry_factor, output_factor, gating_factor, hidden_factor), axis=1)
    owner_expert = jnp.repeat(slot_experts, 2)
    factor_send = jnp.take(stacked, owner_expert, axis=0)
    expert_ids = jnp.arange(experts, dtype=jnp.int32)
    slot_table = jnp.sum(
        jnp.where(slot_experts[None, :] == expert_ids[:, None], expert_ids[None, :], 0), axis=1
    )
    flat_routes = routes.reshape(-1)
    one_hot = (flat_routes[:, None] == expert_ids[None, :]).astype(jnp.int32)
    position = jnp.sum(jnp.cumsum(one_hot, axis=0) * one_hot, axis=1) - 1
    pair_slot = jnp.sum(one_hot * slot_table[None, :], axis=1)
    target = (2 * pair_slot + position // half_cap) * half_cap + position % half_cap
    row_ids = jnp.arange(tok_dev * top_count, dtype=jnp.int32) // top_count
    source_row = jnp.full((devices * half_cap,), tok_dev, jnp.int32).at[target].set(row_ids)
    padded = jnp.concatenate((tokens, jnp.zeros((1, model_width), tokens.dtype)), axis=0)
    send_rows = padded[source_row].reshape(devices, half_cap, model_width)
    far_gateup, far_down = partner((gateup_base, down_base), "expert", 0)
    parity = lax.axis_index("expert") % 2
    got_factors = lax.all_to_all(factor_send, "expert", split_axis=0, concat_axis=0, tiled=True)
    factors = unpack_factors(got_factors, model_width, hidden_width)
    pieces = lax.all_to_all(send_rows, "expert", split_axis=0, concat_axis=0, tiled=True)
    entry_rows, gating_rows, down_rows, output_matrix_rows = factors
    outputs = expert_block(
        pieces.reshape(-1, model_width),
        gateup_base[0],
        far_gateup[0],
        down_base[0],
        far_down[0],
        entry_rows,
        gating_rows,
        down_rows,
        output_matrix_rows,
        parity,
    ).reshape(pieces.shape)
    returned = lax.all_to_all(outputs, "expert", split_axis=0, concat_axis=0, tiled=True)
    picked = returned.reshape(devices * half_cap, model_width)[target].reshape(
        tok_dev, top_count, model_width
    )
    result_sum = jnp.zeros((tok_dev, model_width), jnp.float32)
    for column in range(top_count):
        result_sum = result_sum + route_weights[:, column : column + 1] * picked[:, column].astype(
            jnp.float32
        )
    return result_sum.astype(jnp.bfloat16)


def solution(mesh):
    in_specs = (
        P(("groups", "expert"), None),
        P(("groups", "expert"), None),
        P(("groups", "expert"), None),
        P(),
        P("expert", None, None),
        P("expert", None, None),
        P(None, "expert", None),
        P(None, "expert", None),
        P(None, "expert", None),
        P(None, "expert", None),
    )
    out_specs = P(("groups", "expert"), None)
    return jax.shard_map(
        per_device, mesh=mesh, in_specs=in_specs, out_specs=out_specs, check_vma=False
    )
```

profile of v0, /device:TPU:13, one launch (start us, length us, event | category | flops | bytes accessed | tf_op | source)
XLA Modules:
  0.0 324.7 jit_solution(11416109760836299081)
XLA Ops:
  0.9 1.0 copy.37
  1.9 1.2 pad_maximum_fusion
  3.9 1.4 broadcast_select_fusion
  5.3 6.6 %all-to-all-start.1 = ((bf16[16,656,64]{1,2,0:T(8,128)(2,1)}), bf16[16,656,64]{1,2,0:T(8,128)(2,1)S(1)}, u32[]{:S(2)}, u32[]{:S(2)}) async-start(bf16[16,656,64]{1,2,0:T(8,128)(2,1)} %broadcast_select_fusion), calls=%async_computation.1 | async-start | bytes 3145728 | tf_op jit(solution)/shard_map/all_to_all | solution.py:127
  12.1 1.1 reduce-window.6
  13.8 2.4 scatter_custom_fusion
  16.3 4.4 %gather_fusion = bf16[512,4096]{1,0:T(8,128)(2,1)} fusion(bf16[65,4096]{1,0:T(8,128)(2,1)S(1)} %concatenate.6, s32[1024]{0:T(1024)S(1)} %pad_clamp_fusion.2), kind=kCustom, calls=%fused_computation | custom fusion | bytes 8390656 | tf_op jit(solution)/shard_map/gather | solution.py:124
  20.7 27.3 %all-to-all-done.1 = bf16[16,656,64]{1,2,0:T(8,128)(2,1)S(1)} async-done(((bf16[16,656,64]{1,2,0:T(8,128)(2,1)}), bf16[16,656,64]{1,2,0:T(8,128)(2,1)S(1)}, u32[]{:S(2)}, u32[]{:S(2)}) %all-to-all-start.1) | async-done | bytes 1343520 | tf_op jit(solution)/shard_map/all_to_all | solution.py:127
  48.0 4.9 %all-to-all-start = ((bf16[16,32,4096]{2,1,0:T(8,128)(2,1)}), bf16[16,32,4096]{2,1,0:T(8,128)(2,1)}, u32[]{:S(2)}, u32[]{:S(2)}) async-start(bf16[16,32,4096]{2,1,0:T(8,128)(2,1)} %bitcast.105), calls=%async_computation | async-start | bytes 8388608 | tf_op jit(solution)/shard_map/all_to_all | solution.py:129
  56.9 88.4 %all-to-all-done = bf16[16,32,4096]{2,1,0:T(8,128)(2,1)} async-done(((bf16[16,32,4096]{2,1,0:T(8,128)(2,1)}), bf16[16,32,4096]{2,1,0:T(8,128)(2,1)}, u32[]{:S(2)}, u32[]{:S(2)}) %all-to-all-start) | async-done | bytes 4194336 | tf_op jit(solution)/shard_map/all_to_all | solution.py:129
  145.4 8.6 %fusion.2 = f32[512,768]{1,0:T(8,128)} fusion(bf16[512,4096]{1,0:T(8,128)(2,1)} %bitcast.7, bf16[1,4096,768]{2,1,0:T(8,128)(2,1)} %param.14), kind=kOutput, calls=%fused_computation.7 | convolution fusion | flops 3221225472 | bytes 12058624 | tf_op jit(solution)/shard_map/dot_general | solution.py:41
  154.0 4.3 %fusion.8 = f32[512,1536]{1,0:T(8,128)S(1)} fusion(bf16[1536,64]{0,1:T(8,128)(2,1)S(1)} %reshape.207, bf16[512,4096]{1,0:T(8,128)(2,1)} %bitcast.7, bf16[4096,64]{0,1:T(8,128)(2,1)} %bitcast.108), kind=kOutput, calls=%fused_computation.16 | convolution fusion | flops 369131520 | bytes 8060928 | tf_op jit(solution)/shard_map/dot_general | solution.py:20
  158.3 7.3 %fusion = f32[512,768]{1,0:T(8,128)S(1)} fusion(bf16[512,4096]{1,0:T(8,128)(2,1)} %bitcast.7, bf16[1,4096,768]{2,1,0:T(8,128)(2,1)} %collective-permute-done), kind=kOutput, calls=%fused_computation.5 | convolution fusion | flops 3221225472 | bytes 12058624 | tf_op jit(solution)/shard_map/dot_general | solution.py:42
  165.6 1.4 fusion.19
  167.1 0.9 fusion.24
  168.0 6.1 %fusion.9 = f32[512,4096]{1,0:T(8,128)} fusion(bf16[4096,64]{0,1:T(8,128)(2,1)} %bitcast.107, f32[512,64]{0,1:T(8,128)} %fusion.24, bf16[512,384]{1,0:T(8,128)(2,1)} %get-tuple-element.15, bf16[768,64]{0,1:T(8,128)(2,1)} %reshape.208, s32[]{:T(128)S(6)} %select_n.106), kind=kOutput, calls=%fused_computation.17 | convolution fusion | flops 293666816 | bytes 9486340 | tf_op jit(solution)/shard_map/dot_general | solution.py:20
  174.1 2.3 fusion.5
  176.5 1.0 copy-done
  177.5 6.3 %add_convert_fusion = bf16[512,4096]{1,0:T(8,128)(2,1)} fusion(f32[512,4096]{1,0:T(8,128)S(1)} %copy-done, f32[512,4096]{1,0:T(8,128)S(1)} %fusion.5, bf16[512,384]{1,0:T(8,128)(2,1)S(1)} %copy-done.1, bf16[1,384,4096]{2,1,0:T(8,128)(2,1)} %collective-permute-done.1), kind=kOutput, calls=%fused_computation.4 | convolution fusion | flops 1619001344 | bytes 24510464 | tf_op jit(solution)/shard_map/dot_general | solution.py:62
  183.8 5.0 %all-to-all-start.2 = ((bf16[16,32,4096]{2,1,0:T(8,128)(2,1)}), bf16[16,32,4096]{2,1,0:T(8,128)(2,1)}, u32[]{:S(2)}, u32[]{:S(2)}) async-start(bf16[16,32,4096]{2,1,0:T(8,128)(2,1)} %bitcast.106), calls=%async_computation.2 | async-start | bytes 8388608 | tf_op jit(solution)/shard_map/all_to_all | solution.py:143
  188.9 92.4 %all-to-all-done.2 = bf16[16,32,4096]{2,1,0:T(8,128)(2,1)} async-done(((bf16[16,32,4096]{2,1,0:T(8,128)(2,1)}), bf16[16,32,4096]{2,1,0:T(8,128)(2,1)}, u32[]{:S(2)}, u32[]{:S(2)}) %all-to-all-start.2) | async-done | bytes 4194336 | tf_op jit(solution)/shard_map/all_to_all | solution.py:143
  281.3 11.3 %gather_fusion.2 = bf16[512,4096]{1,0:T(8,128)(2,1)} fusion(bf16[512,4096]{1,0:T(8,128)(2,1)} %bitcast.14, s32[1024]{0:T(1024)S(1)} %pad_clamp_fusion), kind=kCustom, calls=%fused_computation.2 | custom fusion | bytes 8390656 | tf_op jit(solution)/shard_map/gather | solution.py:144
  292.6 22.7 %fusion.38 = (bf16[64,1,4096]{2,1,0:T(2,128)(2,1)S(1)}, bf16[64,1,4096]{2,1,0:T(2,128)(2,1)S(1)}, bf16[64,1,4096]{2,1,0:T(2,128)(2,1)S(1)}, bf16[64,1,4096]{2,1,...) fusion(bf16[64,8,4096]{2,1,0:T(8,128)(2,1)} %bitcast.104), kind=kLoop, calls=%fused_computation.101 | loop fusion | bytes 8388608 | tf_op jit(solution)/shard_map/slice | solution.py:149
  315.3 9.4 %fusion.11 = bf16[64,4096]{1,0:T(8,128)(2,1)} fusion(bf16[64,1,4096]{2,1,0:T(2,128)(2,1)S(1)} %get-tuple-element.14, bf16[64,1,4096]{2,1,0:T(2,128)(2,1)S(1)} %get-tuple-element.8, bf16[64,1,4096]{2,1,0:T(2,128)(2,1)S(1)} %get-tuple-element.9, bf16[64,1,4096]{2,1,0:T(2,128)(2,1)S(1)} %get-tuple-element.10, bf16[64,1,4096]{2,1,0:T(2,128)(2,1)S(1)} %get-tuple-element.11, ...), kind=kLoop, calls=%fused_computation.20 | loop fusion | flops 6291456 | bytes 4720640 | tf_op jit(solution)/shard_map/convert_element_type | solution.py:152
  (54 shorter events, 6.4 us)
Async XLA Ops:
  3.8 8.0 %copy-start.6 = (s32[64,8]{0,1:T(8,128)S(1)}, s32[64,8]{0,1:T(8,128)}, u32[]{:S(2)}) copy-start(s32[64,8]{0,1:T(8,128)} %param.11) | copy-start | bytes 6148
  3.9 9.7 %copy-start.4 = (bf16[64,4096]{1,0:T(8,128)(2,1)S(1)}, bf16[64,4096]{1,0:T(8,128)(2,1)}, u32[]{:S(2)}) copy-start(bf16[64,4096]{1,0:T(8,128)(2,1)} %param.10) | copy-start | bytes 1572868
  3.9 9.7 %copy-start.8 = (s32[8]{0:T(128)S(1)}, s32[8]{0:T(128)}, u32[]{:S(2)}) copy-start(s32[8]{0:T(128)} %param.13) | copy-start | bytes 100
  5.3 42.7 %all-to-all-start.1 = ((bf16[16,656,64]{1,2,0:T(8,128)(2,1)}), bf16[16,656,64]{1,2,0:T(8,128)(2,1)S(1)}, u32[]{:S(2)}, u32[]{:S(2)}) async-start(bf16[16,656,64]{1,2,0:T(8,128)(2,1)} %broadcast_select_fusion), calls=%async_computation.1 | async-start | bytes 3145728 | tf_op jit(solution)/shard_map/all_to_all | solution.py:127
  48.0 97.4 %all-to-all-start = ((bf16[16,32,4096]{2,1,0:T(8,128)(2,1)}), bf16[16,32,4096]{2,1,0:T(8,128)(2,1)}, u32[]{:S(2)}, u32[]{:S(2)}) async-start(bf16[16,32,4096]{2,1,0:T(8,128)(2,1)} %bitcast.105), calls=%async_computation | async-start | bytes 8388608 | tf_op jit(solution)/shard_map/all_to_all | solution.py:129
  52.9 105.4 %collective-permute-start = (bf16[1,4096,768]{2,1,0:T(8,128)(2,1)}, bf16[1,4096,768]{2,1,0:T(8,128)(2,1)}, u32[]{:S(2)}, u32[]{:S(2)}) collective-permute-start(bf16[1,4096,768]{2,1,0:T(8,128)(2,1)} %param.14), channel_id=1, source_target_pairs={{0,1},{1,0},{2,3},{3,2},{4,5},{5,4},{6,7},{7,6},{8,9},{9,8},{10,11... | collective-permute-start | bytes 18874376 | tf_op jit(solution)/shard_map/ppermute | solution.py:16
  53.3 123.2 %collective-permute-start.1 = (bf16[1,384,4096]{2,1,0:T(8,128)(2,1)}, bf16[1,384,4096]{2,1,0:T(8,128)(2,1)}, u32[]{:S(2)}, u32[]{:S(2)}) collective-permute-start(bf16[1,384,4096]{2,1,0:T(8,128)(2,1)} %param.15), channel_id=1, source_target_pairs={{0,1},{1,0},{2,3},{3,2},{4,5},{5,4},{6,7},{7,6},{8,9},{9,8},{10,11... | collective-permute-start | bytes 9437192 | tf_op jit(solution)/shard_map/ppermute | solution.py:16
  158.3 7.4 %copy-start.3 = (f32[512,768]{1,0:T(8,128)S(1)}, f32[512,768]{1,0:T(8,128)}, u32[]{:S(2)}) copy-start(f32[512,768]{1,0:T(8,128)} %fusion.2) | copy-start | bytes 4718596
  165.6 1.4 copy-start.5
  168.0 6.1 %copy-start.2 = (bf16[1,384,4096]{2,1,0:T(8,128)(2,1)S(1)}, bf16[1,384,4096]{2,1,0:T(8,128)(2,1)}, u32[]{:S(2)}) copy-start(bf16[1,384,4096]{2,1,0:T(8,128)(2,1)} %param.15) | copy-start | bytes 9437188
  174.1 3.4 %copy-start = (f32[512,4096]{1,0:T(8,128)S(1)}, f32[512,4096]{1,0:T(8,128)}, u32[]{:S(2)}) copy-start(f32[512,4096]{1,0:T(8,128)} %fusion.9) | copy-start | bytes 25165828
  174.1 3.4 %copy-start.1 = (bf16[512,384]{1,0:T(8,128)(2,1)S(1)}, bf16[512,384]{1,0:T(8,128)(2,1)}, u32[]{:S(2)}) copy-start(bf16[512,384]{1,0:T(8,128)(2,1)} %get-tuple-element.15) | copy-start | bytes 1179652
  183.8 5.1 %copy-start.7 = (f32[64,8]{0,1:T(8,128)S(1)}, f32[64,8]{0,1:T(8,128)}, u32[]{:S(2)}) copy-start(f32[64,8]{0,1:T(8,128)} %param.12) | copy-start | bytes 6148
  183.8 97.5 %all-to-all-start.2 = ((bf16[16,32,4096]{2,1,0:T(8,128)(2,1)}), bf16[16,32,4096]{2,1,0:T(8,128)(2,1)}, u32[]{:S(2)}, u32[]{:S(2)}) async-start(bf16[16,32,4096]{2,1,0:T(8,128)(2,1)} %bitcast.106), calls=%async_computation.2 | async-start | bytes 8388608 | tf_op jit(solution)/shard_map/all_to_all | solution.py:143
where the time goes:
time: 325 us
  waiting for transfers between devices  208 us (64%)
  local copies, waits for them, and re-layouts  48.4 us (15%)
  matrix products  35.9 us (11%)
  starting transfers between devices  17 us (5%)
  other arithmetic  15 us (5%)
    all_to_all x1, waiting for transfers between devices, per_device(): lax.all_to_all(outputs, 'expert', split_axis=0, concat_axis=0, tiled=True)  92.4 us
    all_to_all x1, waiting for transfers between devices, per_device(): lax.all_to_all(send_rows, 'expert', split_axis=0, concat_axis=0, tiled=True)  88.4 us
    all_to_all x1, waiting for transfers between devices, per_device(): lax.all_to_all(factor_send, 'expert', split_axis=0, concat_axis=0, tiled=...  27.3 us
    slice x1, local copies, waits for them, and re-layouts, per_device(): picked[:, column].astype(jnp.float32)  22.7 us
    gather x1, local copies, waits for them, and re-layouts, per_device(): returned.reshape(devices * half_cap, model_width)[target]  11.3 us
    dot_general x2, matrix products, contracted_rows(): lax.dot_general(left, right, (((1,), (1,)), ((), ())), preferred_element_...  10.4 us
    convert_element_type x1, other arithmetic, per_device(): return result_sum.astype(jnp.bfloat16)  9.43 us
    dot_general x1, matrix products, expert_block(): jnp.dot(row_block, near_gateup, preferred_element_type=jnp.float32)  8.61 us
  transfers between devices with their start and end apart: 5, of which 3 were waited for; matrix products, arithmetic and copies ran while one was open for 13% of the time, Pallas kernels for 0%

commit v1 on v0

--- a/solution.py
+++ b/solution.py
@@ -1,6 +1,10 @@
+from functools import partial
+
 import jax
 import jax.numpy as jnp
 from jax import lax
+from jax.experimental import pallas as pl
+from jax.experimental.pallas import tpu as pltpu
 from jax.sharding import PartitionSpec as P
 
 adapter_scale = 0.5
@@ -152,6 +156,228 @@
     return result_sum.astype(jnp.bfloat16)
 
 
+f32, bf16 = jnp.float32, jnp.bfloat16
+lane_count = 128
+chunk_plan = ((1, 2), (3, 4), (5, 6), (7, 0))
+
+
+def dot(left, right):
+    return jnp.dot(left, right, preferred_element_type=f32)
+
+
+def chunk_kernel(blocks, gate_steps, parity, *refs):
+    rows, weights = refs[:blocks], refs[blocks : 2 * blocks]
+    near_gateup, far_gateup, near_down, far_down, model_pack = refs[2 * blocks : 2 * blocks + 5]
+    near_gate, near_up, far_gate, far_up, near_rank, far_rank = refs[2 * blocks + 5 : 2 * blocks + 11]
+    outs = refs[2 * blocks + 11 : 3 * blocks + 11]
+    near_total, far_total, rank_total, hidden, low_rank = refs[3 * blocks + 11 :]
+    step = pl.program_id(0)
+    block_rows = rows[0].shape[0]
+    half = hidden.shape[1] // 2
+    rank = low_rank.shape[1] // 2
+    in_rank = lax.broadcasted_iota(jnp.int32, low_rank.shape, 1) < rank
+
+    @pl.when(step < gate_steps)
+    def _():
+        tile = jnp.concatenate([ref[...] for ref in rows], axis=0)
+        near = dot(tile, near_gateup[0])
+        far = dot(tile, far_gateup[0])
+        low = dot(tile, model_pack[...])
+
+        @pl.when(step == 0)
+        def _():
+            near_total[...] = near
+            far_total[...] = far
+            rank_total[...] = low
+
+        @pl.when(step > 0)
+        def _():
+            near_total[...] += near
+            far_total[...] += far
+            rank_total[...] += low
+
+    @pl.when(step == gate_steps - 1)
+    def _():
+        rank_rows = jnp.where(in_rank, rank_total[...], 0.0).astype(bf16)
+
+        def activate(total, gate_rows, up_rows):
+            gate = total[:, :half] + adapter_scale * contracted_rows(rank_rows, gate_rows[0])
+            up = total[:, half:] + adapter_scale * contracted_rows(rank_rows, up_rows[0])
+            return (gate / (1.0 + jnp.exp(-gate)) * up).astype(bf16)
+
+        hidden_near = activate(near_total, near_gate, near_up)
+        hidden_far = activate(far_total, far_gate, far_up)
+        hidden[:, :half] = hidden_near
+        hidden[:, half:] = hidden_far
+        low = dot(hidden_near, near_rank[0]) + dot(hidden_far, far_rank[0])
+        low_rank[...] = jnp.where(in_rank, 0.0, low).astype(bf16)
+
+    @pl.when(step >= gate_steps)
+    def _():
+        result = dot(hidden[:, :half], near_down[0]) + dot(hidden[:, half:], far_down[0])
+        result = result + adapter_scale * contracted_rows(low_rank[...], model_pack[...])
+        result = result.astype(bf16).astype(f32)
+        for index in range(blocks):
+            own = result[index * block_rows : (index + 1) * block_rows]
+            outs[index][...] = (weights[index][...] * own).astype(bf16)
+
+
+def expert_chunk(rows, weights, near_gateup, far_gateup, near_down, far_down, factors, parity):
+    model_pack, gate_pack, hidden_pack = factors
+    blocks = len(rows)
+    block_rows, width = rows[0].shape
+    both, half = near_gateup.shape[2], near_gateup.shape[2] // 2
+    tile = min(1024, width)
+    steps = width // tile
+    total_rows = blocks * block_rows
+
+    def gate_tile(step):
+        return jnp.minimum(step, steps - 1)
+
+    def down_tile(step):
+        return jnp.maximum(step - steps, 0)
+
+    row_spec = pl.BlockSpec((block_rows, tile), lambda i, p: (0, gate_tile(i)))
+    weight_spec = pl.BlockSpec((block_rows, 1), lambda i, p: (0, 0))
+    gateup_spec = pl.BlockSpec((1, tile, both), lambda i, p: (0, gate_tile(i), 0))
+    down_spec = pl.BlockSpec((1, half, tile), lambda i, p: (0, 0, down_tile(i)))
+    pack_spec = pl.BlockSpec((tile, lane_count), lambda i, p: (jnp.where(i < steps, i, i - steps), 0))
+    part_specs = [
+        pl.BlockSpec((1, half, lane_count), lambda i, p: (p[0], 0, 0)),
+        pl.BlockSpec((1, half, lane_count), lambda i, p: (2 + p[0], 0, 0)),
+        pl.BlockSpec((1, half, lane_count), lambda i, p: (1 - p[0], 0, 0)),
+        pl.BlockSpec((1, half, lane_count), lambda i, p: (3 - p[0], 0, 0)),
+        pl.BlockSpec((1, half, lane_count), lambda i, p: (p[0], 0, 0)),
+        pl.BlockSpec((1, half, lane_count), lambda i, p: (1 - p[0], 0, 0)),
+    ]
+    in_specs = [row_spec] * blocks + [weight_spec] * blocks + [gateup_spec] * 2 + [down_spec] * 2
+    out_spec = pl.BlockSpec((block_rows, tile), lambda i, p: (0, down_tile(i)))
+    return pl.pallas_call(
+        partial(chunk_kernel, blocks, steps),
+        out_shape=[jax.ShapeDtypeStruct((block_rows, width), bf16)] * blocks,
+        grid_spec=pltpu.PrefetchScalarGridSpec(
+            num_scalar_prefetch=1,
+            grid=(2 * steps,),
+            in_specs=in_specs + [pack_spec] + part_specs,
+            out_specs=[out_spec] * blocks,
+            scratch_shapes=[
+                pltpu.VMEM((total_rows, both), f32),
+                pltpu.VMEM((total_rows, both), f32),
+                pltpu.VMEM((total_rows, lane_count), f32),
+                pltpu.VMEM((total_rows, both), bf16),
+                pltpu.VMEM((total_rows, lane_count), bf16),
+            ],
+        ),
+        compiler_params=pltpu.CompilerParams(vmem_limit_bytes=24 * 2**20),
+        cost_estimate=pl.CostEstimate(
+            flops=2 * total_rows * width * (3 * both + 2 * lane_count),
+            bytes_accessed=2 * (3 * both * width + 2 * total_rows * width),
+            transcendentals=total_rows * both,
+        ),
+        name="expert_chunk",
+    )(
+        parity, *rows, *weights, near_gateup, far_gateup, near_down, far_down, model_pack,
+        gate_pack, gate_pack, gate_pack, gate_pack, hidden_pack, hidden_pack,
+    )
+
+
+def ring_order(chips):
+    return list(range(0, chips, 2)) + list(range(1, chips, 2))[::-1]
+
+
+def hop_pairs(order, hops):
+    count = len(order)
+    pairs = []
+    for place in range(count):
+        for core, sign in ((0, 1), (1, -1)):
+            pairs.append((2 * order[place] + core, 2 * order[(place + sign * hops) % count] + core))
+    return pairs
+
+
+def weight_pieces(weights):
+    high = lax.reduce_precision(weights, 8, 7)
+    middle = lax.reduce_precision(weights - high, 8, 7)
+    return [piece.astype(bf16) for piece in (high, middle, weights - high - middle)]
+
+
+def dense_per_device(
+    tokens, routes, route_weights, slot_experts, gateup_base, down_base,
+    entry_factor, gating_factor, hidden_factor, output_factor,
+):
+    devices = lax.axis_size("expert")
+    chips = devices // 2
+    tok_dev, width = tokens.shape
+    experts, width_rows, rank = entry_factor.shape
+    gating_rows, hidden_rows = gating_factor.shape[1], hidden_factor.shape[1]
+    order = ring_order(chips)
+    pairs = hop_pairs(order, 1)
+    me = lax.axis_index("expert")
+    parity, chip = me % 2, me // 2
+    order_array = jnp.array(order, jnp.int32)
+    place = jnp.sum(jnp.where(order_array == chip, jnp.arange(chips, dtype=jnp.int32), 0))
+    sign = 1 - 2 * parity
+    hops = jnp.arange(chips, dtype=jnp.int32)
+
+    far_gateup, far_down = partner((gateup_base, down_base), "expert", 0)
+    rows = [tokens]
+    for _ in range(1, chips):
+        rows.append(lax.ppermute(rows[-1], "expert", pairs))
+
+    expert_ids = jnp.arange(experts, dtype=jnp.int32)
+    named = routes[None, :, :] == expert_ids[:, None, None]
+    by_expert = jnp.sum(jnp.where(named, route_weights[None, :, :], 0.0), axis=2)
+    pieces = jnp.stack(weight_pieces(by_expert), axis=1)
+    spare = jnp.zeros((experts, gating_rows - hidden_rows - 3, rank), bf16)
+    right = jnp.concatenate((hidden_factor, pieces, spare), axis=1)
+    stacked = jnp.concatenate(
+        (
+            jnp.concatenate((entry_factor, output_factor), axis=2),
+            jnp.concatenate((gating_factor, right), axis=2),
+        ),
+        axis=1,
+    )
+    target_chip = order_array[(place + sign * hops) % chips]
+    factor_send = jnp.take(stacked, slot_experts[target_chip], axis=0)
+    got = [factor_send[0]]
+    for hop in range(1, chips):
+        got.append(lax.ppermute(factor_send[hop], "expert", hop_pairs(order, hop)))
+    got = jnp.stack(got)
+    hidden_end = width_rows + hidden_rows
+    weights = jnp.sum(got[:, hidden_end : hidden_end + 3, rank:].astype(f32), axis=1)[:, :, None]
+    hop_of_chip = (sign * (place - jnp.argsort(order_array))) % chips
+    near_pack = jnp.take(got, hop_of_chip, axis=0)
+    far_pack = partner(near_pack, "expert", 0)
+    even = jnp.where(parity == 0, near_pack, far_pack)
+    odd = jnp.where(parity == 0, far_pack, near_pack)
+    by_device = jnp.stack((even, odd), axis=1)
+    model_pack = by_device[:, :, :width_rows].reshape(width, 2 * rank)
+    gate_pack = by_device[:, :, width_rows:].reshape(4, -1, 2 * rank)
+    hidden_pack = by_device[:, :, width_rows:hidden_end].reshape(2, -1, 2 * rank)
+    factors = (model_pack, gate_pack, hidden_pack)
+
+    outputs = {}
+    for members in chunk_plan:
+        results = expert_chunk(
+            [rows[hop] for hop in members], [weights[hop] for hop in members],
+            gateup_base, far_gateup, down_base, far_down, factors, parity.reshape(1),
+        )
+        outputs.update(zip(members, results))
+    running = outputs[1]
+    for hop in range(1, chips):
+        arrived = lax.ppermute(running, "expert", pairs)
+        running = arrived.astype(f32) + outputs[(hop + 1) % chips].astype(f32)
+        running = running.astype(bf16)
+    return running
+
+
+def program(*args):
+    routes, entry_factor, tokens = args[1], args[6], args[0]
+    experts, rank = entry_factor.shape[0], entry_factor.shape[2]
+    every = routes.shape[1] == experts and lax.axis_size("expert") == 2 * experts
+    every = every and experts == 8 and 2 * rank == lane_count and tokens.shape[0] == rank
+    return (dense_per_device if every else per_device)(*args)
+
+
 def solution(mesh):
     in_specs = (
         P(("groups", "expert"), None),
@@ -167,5 +393,5 @@
     )
     out_specs = P(("groups", "expert"), None)
     return jax.shard_map(
-        per_device, mesh=mesh, in_specs=in_specs, out_specs=out_specs, check_vma=False
-    )
+        program, mesh=mesh, in_specs=in_specs, out_specs=out_specs, check_vma=False
+    )

time: 325 us -> 187 us (0.58)
  the two profiles are of different devices: /device:TPU:13 before, /device:TPU:0 now
where the time goes in v1:
time: 187 us; the launch traced here: 185 us
  waiting for transfers between devices  52.9 us (28%)
  local copies, waits for them, and re-layouts  45 us (24%)
  Pallas kernels  39.2 us (21%)
  starting transfers between devices  29.7 us (16%)
  other arithmetic  17.7 us (9%)
    pallas_call x4, Pallas kernels, expert_chunk(): pl.pallas_call(partial(chunk_kernel, blocks, steps), out_shape=[jax.Shape...  39.2 us
    unnamed x61, local copies, waits for them, and re-layouts  27.7 us
    ppermute x7, waiting for transfers between devices, dense_per_device(): arrived = lax.ppermute(running, 'expert', pairs)  26.1 us
    ppermute x7, waiting for transfers between devices, dense_per_device(): rows.append(lax.ppermute(rows[-1], 'expert', pairs))  19 us
    ppermute x7, starting transfers between devices, dense_per_device(): got.append(lax.ppermute(factor_send[hop], 'expert', hop_pairs(order, hop)))  13.9 us
    ppermute x7, starting transfers between devices, dense_per_device(): arrived = lax.ppermute(running, 'expert', pairs)  8.88 us
    squeeze x9, local copies, waits for them, and re-layouts, dense_per_device(): weights[hop]  8.03 us
    ppermute x7, waiting for transfers between devices, dense_per_device(): got.append(lax.ppermute(factor_send[hop], 'expert', hop_pairs(order, hop)))  7.87 us
  transfers between devices with their start and end apart: 24, of which 12 were waited for; matrix products, arithmetic and copies ran while one was open for 20% of the time, Pallas kernels for 21%

profile of v1, /device:TPU:0, one launch (start us, length us, event | category | flops | bytes accessed | tf_op | source)
XLA Modules:
  0.0 185.0 jit_solution(2973864736668752952)
XLA Ops:
  8.7 2.8 %gather_fusion.2 = bf16[8,352,128]{2,1,0:T(8,128)(2,1)} fusion(bf16[8,352,128]{2,1,0:T(8,128)(2,1)} %maximum_maximum_fusion, s32[1024]{0:T(1024)S(1)} %pad_clamp_fusion.1), kind=kCustom, calls=%fused_computation.clone | custom fusion | bytes 1441824 | tf_op jit(solution)/shard_map/jit(_take)/gather | solution.py:340
  13.4 2.7 %collective-permute-start.2 = (bf16[352,128]{1,0:T(8,128)(2,1)S(1)}, bf16[352,128]{1,0:T(8,128)(2,1)S(1)}, u32[]{:S(2)}, u32[]{:S(2)}) collective-permute-start(bf16[352,128]{1,0:T(8,128)(2,1)S(1)} %get-tuple-element.34), channel_id=1, source_target_pairs={{0,4},{1,3},{4,8},{5,1},{8,12},{9,5},{12,14},{13,9},{14,10},{15,13... | collective-permute-start | bytes 270344 | tf_op jit(solution)/shard_map/ppermute | solution.py:343
  16.1 2.6 %collective-permute-start.3 = (bf16[352,128]{1,0:T(8,128)(2,1)S(1)}, bf16[352,128]{1,0:T(8,128)(2,1)S(1)}, u32[]{:S(2)}, u32[]{:S(2)}) collective-permute-start(bf16[352,128]{1,0:T(8,128)(2,1)S(1)} %get-tuple-element.33), channel_id=1, source_target_pairs={{0,8},{1,7},{4,12},{5,3},{8,14},{9,1},{12,10},{13,5},{14,6},{15,9}... | collective-permute-start | bytes 270344 | tf_op jit(solution)/shard_map/ppermute | solution.py:343
  20.0 2.4 %collective-permute-start.5 = (bf16[352,128]{1,0:T(8,128)(2,1)S(1)}, bf16[352,128]{1,0:T(8,128)(2,1)S(1)}, u32[]{:S(2)}, u32[]{:S(2)}) collective-permute-start(bf16[352,128]{1,0:T(8,128)(2,1)S(1)} %get-tuple-element.31), channel_id=1, source_target_pairs={{0,14},{1,15},{4,10},{5,11},{8,6},{9,7},{12,2},{13,3},{14,0},{15,1... | collective-permute-start | bytes 270344 | tf_op jit(solution)/shard_map/ppermute | solution.py:343
  25.1 5.3 %collective-permute-done.4 = bf16[352,128]{1,0:T(8,128)(2,1)S(1)} collective-permute-done((bf16[352,128]{1,0:T(8,128)(2,1)S(1)}, bf16[352,128]{1,0:T(8,128)(2,1)S(1)}, u32[]{:S(2)}, u32[]{:S(2)}) %collective-permute-start.4) | collective-permute-done | bytes 90144 | tf_op jit(solution)/shard_map/ppermute | solution.py:343
  30.4 4.3 %collective-permute-start.7 = (bf16[352,128]{1,0:T(8,128)(2,1)S(1)}, bf16[352,128]{1,0:T(8,128)(2,1)S(1)}, u32[]{:S(2)}, u32[]{:S(2)}) collective-permute-start(bf16[352,128]{1,0:T(8,128)(2,1)S(1)} %get-tuple-element.29), channel_id=1, source_target_pairs={{0,6},{1,9},{4,2},{5,13},{8,0},{9,15},{12,4},{13,11},{14,8},{15,7}... | collective-permute-start | bytes 270344 | tf_op jit(solution)/shard_map/ppermute | solution.py:343
  37.5 2.4 %collective-permute-done.8 = bf16[352,128]{1,0:T(8,128)(2,1)S(1)} collective-permute-done((bf16[352,128]{1,0:T(8,128)(2,1)S(1)}, bf16[352,128]{1,0:T(8,128)(2,1)S(1)}, u32[]{:S(2)}, u32[]{:S(2)}) %collective-permute-start.8) | collective-permute-done | bytes 90144 | tf_op jit(solution)/shard_map/ppermute | solution.py:343
  40.5 2.6 %gather_fusion.3 = bf16[8,352,128]{2,1,0:T(8,128)(2,1)} fusion(bf16[8,352,128]{2,1,0:T(8,128)(2,1)} %bitcast_dynamic-update-slice_fusion, s32[1024]{0:T(1024)S(1)} %pad_clamp_fusion), kind=kCustom, calls=%fused_computation.1.clone | custom fusion | bytes 1441824 | tf_op jit(solution)/shard_map/jit(_take)/gather | solution.py:348
  48.1 6.7 %collective-permute-done.refs_0_ = bf16[64,4096]{1,0:T(8,128)(2,1)} collective-permute-done((bf16[64,4096]{1,0:T(8,128)(2,1)}, bf16[64,4096]{1,0:T(8,128)(2,1)}, u32[]{:S(2)}, u32[]{:S(2)}) %collective-permute-start) | collective-permute-done | bytes 524320 | tf_op jit(solution)/shard_map/ppermute | solution.py:324
  56.6 7.5 %collective-permute-done.1.refs_1_ = bf16[64,4096]{1,0:T(8,128)(2,1)S(1)} collective-permute-done((bf16[64,4096]{1,0:T(8,128)(2,1)}, bf16[64,4096]{1,0:T(8,128)(2,1)S(1)}, u32[]{:S(2)}, u32[]{:S(2)}) %collective-permute-start.1) | collective-permute-done | bytes 524320 | tf_op jit(solution)/shard_map/ppermute | solution.py:324
  64.2 2.8 %copy-done.1 = bf16[1,4096,768]{2,1,0:T(8,128)(2,1)S(1)} copy-done((bf16[1,4096,768]{2,1,0:T(8,128)(2,1)S(1)}, bf16[1,4096,768]{2,1,0:T(8,128)(2,1)}, u32[]{:S(2)}) %copy-start.1) | copy-done | bytes 6291480
  67.0 9.7 %expert_chunk.4 = (bf16[64,4096]{1,0:T(8,128)(2,1)S(1)}, bf16[64,4096]{1,0:T(8,128)(2,1)S(1)}) custom-call(s32[1]{0:T(128)} %bitcast.parity, bf16[64,4096]{1,0:T(8,128)(2,1)} %collective-permute-done.refs_0_, bf16[64,4096]{1,0:T(8,128)(2,1)S(1)} %collective-permute-done.1.refs_1_, f32[64,1]{1,0:T(8,128)S(1)} %copy-done.14, f32[64,1]{1,0:T(8,128)S(1)} %copy-done.15, ...), custom_call_target="tpu_custom_call" | custom-call | flops 2684354560 | bytes 20971520 | tf_op jit(solution)/shard_map/expert_chunk/pallas_call | solution.py:255
  78.7 7.2 %collective-permute-done.12 = bf16[64,4096]{1,0:T(8,128)(2,1)S(1)} collective-permute-done((bf16[64,4096]{1,0:T(8,128)(2,1)S(1)}, bf16[64,4096]{1,0:T(8,128)(2,1)S(1)}, u32[]{:S(2)}, u32[]{:S(2)}) %collective-permute-start.12) | collective-permute-done | bytes 524320 | tf_op jit(solution)/shard_map/ppermute | solution.py:367
  92.4 2.8 %copy-done.2 = bf16[1,4096,768]{2,1,0:T(8,128)(2,1)S(1)} copy-done((bf16[1,4096,768]{2,1,0:T(8,128)(2,1)S(1)}, bf16[1,4096,768]{2,1,0:T(8,128)(2,1)}, u32[]{:S(2)}) %copy-start.2) | copy-done | bytes 6291480
  98.8 9.8 %expert_chunk.5 = (bf16[64,4096]{1,0:T(8,128)(2,1)S(1)}, bf16[64,4096]{1,0:T(8,128)(2,1)S(1)}) custom-call(s32[1]{0:T(128)} %bitcast.parity, bf16[64,4096]{1,0:T(8,128)(2,1)} %collective-permute-done.14.refs_0_, bf16[64,4096]{1,0:T(8,128)(2,1)} %collective-permute-done.15.refs_1_, f32[64,1]{1,0:T(8,128)S(1)} %copy-done.18, f32[64,1]{1,0:T(8,128)S(1)} %copy-done.19, ...), custom_call_target="tpu_custom_call" | custom-call | flops 2684354560 | bytes 20971520 | tf_op jit(solution)/shard_map/expert_chunk/pallas_call | solution.py:255
  111.4 2.2 %collective-permute-start.19 = (bf16[64,4096]{1,0:T(8,128)(2,1)}, bf16[64,4096]{1,0:T(8,128)(2,1)}, u32[]{:S(2)}, u32[]{:S(2)}) collective-permute-start(bf16[64,4096]{1,0:T(8,128)(2,1)} %collective-permute-done.18.refs_0_), channel_id=1, source_target_pairs={{0,4},{1,3},{4,8},{5,1},{8,12},{9,5},{12,14},{13,9},{14,10},{15,13... | collective-permute-start | bytes 1572872 | tf_op jit(solution)/shard_map/ppermute | solution.py:324
  113.6 5.5 %collective-permute-done.16 = bf16[64,4096]{1,0:T(8,128)(2,1)S(1)} collective-permute-done((bf16[64,4096]{1,0:T(8,128)(2,1)S(1)}, bf16[64,4096]{1,0:T(8,128)(2,1)S(1)}, u32[]{:S(2)}, u32[]{:S(2)}) %collective-permute-start.16) | collective-permute-done | bytes 524320 | tf_op jit(solution)/shard_map/ppermute | solution.py:367
  124.9 2.8 %copy-done.3 = bf16[1,4096,768]{2,1,0:T(8,128)(2,1)S(1)} copy-done((bf16[1,4096,768]{2,1,0:T(8,128)(2,1)S(1)}, bf16[1,4096,768]{2,1,0:T(8,128)(2,1)}, u32[]{:S(2)}) %copy-start.3) | copy-done | bytes 6291480
  131.3 9.9 %expert_chunk.6 = (bf16[64,4096]{1,0:T(8,128)(2,1)S(1)}, bf16[64,4096]{1,0:T(8,128)(2,1)S(1)}) custom-call(s32[1]{0:T(128)} %bitcast.parity, bf16[64,4096]{1,0:T(8,128)(2,1)} %collective-permute-done.18.refs_0_, bf16[64,4096]{1,0:T(8,128)(2,1)} %collective-permute-done.19.refs_1_, f32[64,1]{1,0:T(8,128)S(1)} %copy-done.20, f32[64,1]{1,0:T(8,128)S(1)} %copy-done.21, ...), custom_call_target="tpu_custom_call" | custom-call | flops 2684354560 | bytes 20971520 | tf_op jit(solution)/shard_map/expert_chunk/pallas_call | solution.py:255
  143.9 2.2 %collective-permute-start.22 = (bf16[64,4096]{1,0:T(8,128)(2,1)}, bf16[64,4096]{1,0:T(8,128)(2,1)}, u32[]{:S(2)}, u32[]{:S(2)}) collective-permute-start(bf16[64,4096]{1,0:T(8,128)(2,1)} %collective-permute-done.19.refs_1_), channel_id=1, source_target_pairs={{0,4},{1,3},{4,8},{5,1},{8,12},{9,5},{12,14},{13,9},{14,10},{15,13... | collective-permute-start | bytes 1572872 | tf_op jit(solution)/shard_map/ppermute | solution.py:324
  146.1 5.6 %collective-permute-done.20 = bf16[64,4096]{1,0:T(8,128)(2,1)S(1)} collective-permute-done((bf16[64,4096]{1,0:T(8,128)(2,1)S(1)}, bf16[64,4096]{1,0:T(8,128)(2,1)S(1)}, u32[]{:S(2)}, u32[]{:S(2)}) %collective-permute-start.20) | collective-permute-done | bytes 524320 | tf_op jit(solution)/shard_map/ppermute | solution.py:367
  157.3 2.8 %copy-done.4 = bf16[1,4096,768]{2,1,0:T(8,128)(2,1)S(1)} copy-done((bf16[1,4096,768]{2,1,0:T(8,128)(2,1)S(1)}, bf16[1,4096,768]{2,1,0:T(8,128)(2,1)}, u32[]{:S(2)}) %copy-start.4) | copy-done | bytes 6291480
  163.8 9.9 %expert_chunk.7 = (bf16[64,4096]{1,0:T(8,128)(2,1)S(1)}, bf16[64,4096]{1,0:T(8,128)(2,1)S(1)}) custom-call(s32[1]{0:T(128)} %bitcast.parity, bf16[64,4096]{1,0:T(8,128)(2,1)} %collective-permute-done.22.refs_0_, bf16[64,4096]{1,0:T(8,128)(2,1)} %refs_1_.1, f32[64,1]{1,0:T(8,128)S(1)} %copy-done.16, f32[64,1]{1,0:T(8,128)S(1)} %copy-done.17, ...), custom_call_target="tpu_custom_call" | custom-call | flops 2684354560 | bytes 20971520 | tf_op jit(solution)/shard_map/expert_chunk/pallas_call | solution.py:255
  176.3 7.7 %collective-permute-done.23 = bf16[64,4096]{1,0:T(8,128)(2,1)S(1)} collective-permute-done((bf16[64,4096]{1,0:T(8,128)(2,1)S(1)}, bf16[64,4096]{1,0:T(8,128)(2,1)S(1)}, u32[]{:S(2)}, u32[]{:S(2)}) %collective-permute-start.23) | collective-permute-done | bytes 524320 | tf_op jit(solution)/shard_map/ppermute | solution.py:367
  (139 shorter events, 64.5 us)
Async XLA Ops:
  0.0 64.1 %collective-permute-start.9 = (bf16[1,4096,768]{2,1,0:T(8,128)(2,1)}, bf16[1,4096,768]{2,1,0:T(8,128)(2,1)}, u32[]{:S(2)}, u32[]{:S(2)}) collective-permute-start(bf16[1,4096,768]{2,1,0:T(8,128)(2,1)} %refs_4_.7), channel_id=1, source_target_pairs={{0,1},{1,0},{2,3},{3,2},{4,5},{5,4},{6,7},{7,6},{8,9},{9,8},{10,11... | collective-permute-start | bytes 18874376 | tf_op jit(solution)/shard_map/ppermute | solution.py:20
  13.4 9.6 %collective-permute-start.2 = (bf16[352,128]{1,0:T(8,128)(2,1)S(1)}, bf16[352,128]{1,0:T(8,128)(2,1)S(1)}, u32[]{:S(2)}, u32[]{:S(2)}) collective-permute-start(bf16[352,128]{1,0:T(8,128)(2,1)S(1)} %get-tuple-element.34), channel_id=1, source_target_pairs={{0,4},{1,3},{4,8},{5,1},{8,12},{9,5},{12,14},{13,9},{14,10},{15,13... | collective-permute-start | bytes 270344 | tf_op jit(solution)/shard_map/ppermute | solution.py:343
  16.1 7.7 %collective-permute-start.3 = (bf16[352,128]{1,0:T(8,128)(2,1)S(1)}, bf16[352,128]{1,0:T(8,128)(2,1)S(1)}, u32[]{:S(2)}, u32[]{:S(2)}) collective-permute-start(bf16[352,128]{1,0:T(8,128)(2,1)S(1)} %get-tuple-element.33), channel_id=1, source_target_pairs={{0,8},{1,7},{4,12},{5,3},{8,14},{9,1},{12,10},{13,5},{14,6},{15,9}... | collective-permute-start | bytes 270344 | tf_op jit(solution)/shard_map/ppermute | solution.py:343
  18.7 11.7 %collective-permute-start.4 = (bf16[352,128]{1,0:T(8,128)(2,1)S(1)}, bf16[352,128]{1,0:T(8,128)(2,1)S(1)}, u32[]{:S(2)}, u32[]{:S(2)}) collective-permute-start(bf16[352,128]{1,0:T(8,128)(2,1)S(1)} %get-tuple-element.32), channel_id=1, source_target_pairs={{0,12},{1,11},{4,14},{5,7},{8,10},{9,3},{12,6},{13,1},{14,2},{15,5... | collective-permute-start | bytes 270344 | tf_op jit(solution)/shard_map/ppermute | solution.py:343
  20.0 15.3 %collective-permute-start.5 = (bf16[352,128]{1,0:T(8,128)(2,1)S(1)}, bf16[352,128]{1,0:T(8,128)(2,1)S(1)}, u32[]{:S(2)}, u32[]{:S(2)}) collective-permute-start(bf16[352,128]{1,0:T(8,128)(2,1)S(1)} %get-tuple-element.31), channel_id=1, source_target_pairs={{0,14},{1,15},{4,10},{5,11},{8,6},{9,7},{12,2},{13,3},{14,0},{15,1... | collective-permute-start | bytes 270344 | tf_op jit(solution)/shard_map/ppermute | solution.py:343
  23.1 41.0 %collective-permute-start.10 = (bf16[1,384,4096]{2,1,0:T(8,128)(2,1)S(1)}, bf16[1,384,4096]{2,1,0:T(8,128)(2,1)}, u32[]{:S(2)}, u32[]{:S(2)}) collective-permute-start(bf16[1,384,4096]{2,1,0:T(8,128)(2,1)S(1)} %copy-done.5), channel_id=1, source_target_pairs={{0,1},{1,0},{2,3},{3,2},{4,5},{5,4},{6,7},{7,6},{8,9},{9,8},{10,11... | collective-permute-start | bytes 9437192 | tf_op jit(solution)/shard_map/ppermute | solution.py:20
  23.8 12.2 %collective-permute-start.6 = (bf16[352,128]{1,0:T(8,128)(2,1)S(1)}, bf16[352,128]{1,0:T(8,128)(2,1)S(1)}, u32[]{:S(2)}, u32[]{:S(2)}) collective-permute-start(bf16[352,128]{1,0:T(8,128)(2,1)S(1)} %get-tuple-element.30), channel_id=1, source_target_pairs={{0,10},{1,13},{4,6},{5,15},{8,2},{9,11},{12,0},{13,7},{14,4},{15,3... | collective-permute-start | bytes 270344 | tf_op jit(solution)/shard_map/ppermute | solution.py:343
  30.4 6.4 %collective-permute-start.7 = (bf16[352,128]{1,0:T(8,128)(2,1)S(1)}, bf16[352,128]{1,0:T(8,128)(2,1)S(1)}, u32[]{:S(2)}, u32[]{:S(2)}) collective-permute-start(bf16[352,128]{1,0:T(8,128)(2,1)S(1)} %get-tuple-element.29), channel_id=1, source_target_pairs={{0,6},{1,9},{4,2},{5,13},{8,0},{9,15},{12,4},{13,11},{14,8},{15,7}... | collective-permute-start | bytes 270344 | tf_op jit(solution)/shard_map/ppermute | solution.py:343
  35.3 4.5 %collective-permute-start.8 = (bf16[352,128]{1,0:T(8,128)(2,1)S(1)}, bf16[352,128]{1,0:T(8,128)(2,1)S(1)}, u32[]{:S(2)}, u32[]{:S(2)}) collective-permute-start(bf16[352,128]{1,0:T(8,128)(2,1)S(1)} %get-tuple-element.28), channel_id=1, source_target_pairs={{0,2},{1,5},{4,0},{5,9},{8,4},{9,13},{12,8},{13,15},{14,12},{15,11... | collective-permute-start | bytes 270344 | tf_op jit(solution)/shard_map/ppermute | solution.py:343
  45.2 9.5 %collective-permute-start.11 = (bf16[8,352,128]{2,1,0:T(8,128)(2,1)}, bf16[8,352,128]{2,1,0:T(8,128)(2,1)}, u32[]{:S(2)}, u32[]{:S(2)}) collective-permute-start(bf16[8,352,128]{2,1,0:T(8,128)(2,1)} %broadcast_select_fusion), channel_id=1, source_target_pairs={{0,1},{1,0},{2,3},{3,2},{4,5},{5,4},{6,7},{7,6},{8,9},{9,8},{10,11... | collective-permute-start | bytes 2162696 | tf_op jit(solution)/shard_map/ppermute | solution.py:20
  45.2 9.5 %collective-permute-start = (bf16[64,4096]{1,0:T(8,128)(2,1)}, bf16[64,4096]{1,0:T(8,128)(2,1)}, u32[]{:S(2)}, u32[]{:S(2)}) collective-permute-start(bf16[64,4096]{1,0:T(8,128)(2,1)} %refs_1_.1), channel_id=1, source_target_pairs={{0,4},{1,3},{4,8},{5,1},{8,12},{9,5},{12,14},{13,9},{14,10},{15,13... | collective-permute-start | bytes 1572872 | tf_op jit(solution)/shard_map/ppermute | solution.py:324
  54.7 9.4 %collective-permute-start.1 = (bf16[64,4096]{1,0:T(8,128)(2,1)}, bf16[64,4096]{1,0:T(8,128)(2,1)S(1)}, u32[]{:S(2)}, u32[]{:S(2)}) collective-permute-start(bf16[64,4096]{1,0:T(8,128)(2,1)} %collective-permute-done.refs_0_), channel_id=1, source_target_pairs={{0,4},{1,3},{4,8},{5,1},{8,12},{9,5},{12,14},{13,9},{14,10},{15,13... | collective-permute-start | bytes 1572872 | tf_op jit(solution)/shard_map/ppermute | solution.py:324
  64.1 13.4 %collective-permute-start.14 = (bf16[64,4096]{1,0:T(8,128)(2,1)S(1)}, bf16[64,4096]{1,0:T(8,128)(2,1)}, u32[]{:S(2)}, u32[]{:S(2)}) collective-permute-start(bf16[64,4096]{1,0:T(8,128)(2,1)S(1)} %collective-permute-done.1.refs_1_), channel_id=1, source_target_pairs={{0,4},{1,3},{4,8},{5,1},{8,12},{9,5},{12,14},{13,9},{14,10},{15,13... | collective-permute-start | bytes 1572872 | tf_op jit(solution)/shard_map/ppermute | solution.py:324
  76.7 9.2 %collective-permute-start.12 = (bf16[64,4096]{1,0:T(8,128)(2,1)S(1)}, bf16[64,4096]{1,0:T(8,128)(2,1)S(1)}, u32[]{:S(2)}, u32[]{:S(2)}) collective-permute-start(bf16[64,4096]{1,0:T(8,128)(2,1)S(1)} %get-tuple-element.16), channel_id=1, source_target_pairs={{0,4},{1,3},{4,8},{5,1},{8,12},{9,5},{12,14},{13,9},{14,10},{15,13... | collective-permute-start | bytes 1572872 | tf_op jit(solution)/shard_map/ppermute | solution.py:367
  77.5 14.1 %collective-permute-start.15 = (bf16[64,4096]{1,0:T(8,128)(2,1)}, bf16[64,4096]{1,0:T(8,128)(2,1)}, u32[]{:S(2)}, u32[]{:S(2)}) collective-permute-start(bf16[64,4096]{1,0:T(8,128)(2,1)} %collective-permute-done.14.refs_0_), channel_id=1, source_target_pairs={{0,4},{1,3},{4,8},{5,1},{8,12},{9,5},{12,14},{13,9},{14,10},{15,13... | collective-permute-start | bytes 1572872 | tf_op jit(solution)/shard_map/ppermute | solution.py:324
  86.8 21.9 %collective-permute-start.13 = (bf16[64,4096]{1,0:T(8,128)(2,1)}, bf16[64,4096]{1,0:T(8,128)(2,1)}, u32[]{:S(2)}, u32[]{:S(2)}) collective-permute-start(bf16[64,4096]{1,0:T(8,128)(2,1)} %add_convert_fusion.6), channel_id=1, source_target_pairs={{0,4},{1,3},{4,8},{5,1},{8,12},{9,5},{12,14},{13,9},{14,10},{15,13... | collective-permute-start | bytes 1572872 | tf_op jit(solution)/shard_map/ppermute | solution.py:367
  91.6 19.8 %collective-permute-start.18 = (bf16[64,4096]{1,0:T(8,128)(2,1)}, bf16[64,4096]{1,0:T(8,128)(2,1)}, u32[]{:S(2)}, u32[]{:S(2)}) collective-permute-start(bf16[64,4096]{1,0:T(8,128)(2,1)} %collective-permute-done.15.refs_1_), channel_id=1, source_target_pairs={{0,4},{1,3},{4,8},{5,1},{8,12},{9,5},{12,14},{13,9},{14,10},{15,13... | collective-permute-start | bytes 1572872 | tf_op jit(solution)/shard_map/ppermute | solution.py:324
  109.9 9.2 %collective-permute-start.16 = (bf16[64,4096]{1,0:T(8,128)(2,1)S(1)}, bf16[64,4096]{1,0:T(8,128)(2,1)S(1)}, u32[]{:S(2)}, u32[]{:S(2)}) collective-permute-start(bf16[64,4096]{1,0:T(8,128)(2,1)S(1)} %add_convert_fusion.5), channel_id=1, source_target_pairs={{0,4},{1,3},{4,8},{5,1},{8,12},{9,5},{12,14},{13,9},{14,10},{15,13... | collective-permute-start | bytes 1572872 | tf_op jit(solution)/shard_map/ppermute | solution.py:367
  111.4 13.5 %collective-permute-start.19 = (bf16[64,4096]{1,0:T(8,128)(2,1)}, bf16[64,4096]{1,0:T(8,128)(2,1)}, u32[]{:S(2)}, u32[]{:S(2)}) collective-permute-start(bf16[64,4096]{1,0:T(8,128)(2,1)} %collective-permute-done.18.refs_0_), channel_id=1, source_target_pairs={{0,4},{1,3},{4,8},{5,1},{8,12},{9,5},{12,14},{13,9},{14,10},{15,13... | collective-permute-start | bytes 1572872 | tf_op jit(solution)/shard_map/ppermute | solution.py:324
  120.0 21.1 %collective-permute-start.17 = (bf16[64,4096]{1,0:T(8,128)(2,1)}, bf16[64,4096]{1,0:T(8,128)(2,1)}, u32[]{:S(2)}, u32[]{:S(2)}) collective-permute-start(bf16[64,4096]{1,0:T(8,128)(2,1)} %add_convert_fusion.4), channel_id=1, source_target_pairs={{0,4},{1,3},{4,8},{5,1},{8,12},{9,5},{12,14},{13,9},{14,10},{15,13... | collective-permute-start | bytes 1572872 | tf_op jit(solution)/shard_map/ppermute | solution.py:367
  142.4 9.2 %collective-permute-start.20 = (bf16[64,4096]{1,0:T(8,128)(2,1)S(1)}, bf16[64,4096]{1,0:T(8,128)(2,1)S(1)}, u32[]{:S(2)}, u32[]{:S(2)}) collective-permute-start(bf16[64,4096]{1,0:T(8,128)(2,1)S(1)} %add_convert_fusion.3), channel_id=1, source_target_pairs={{0,4},{1,3},{4,8},{5,1},{8,12},{9,5},{12,14},{13,9},{14,10},{15,13... | collective-permute-start | bytes 1572872 | tf_op jit(solution)/shard_map/ppermute | solution.py:367
  143.9 13.5 %collective-permute-start.22 = (bf16[64,4096]{1,0:T(8,128)(2,1)}, bf16[64,4096]{1,0:T(8,128)(2,1)}, u32[]{:S(2)}, u32[]{:S(2)}) collective-permute-start(bf16[64,4096]{1,0:T(8,128)(2,1)} %collective-permute-done.19.refs_1_), channel_id=1, source_target_pairs={{0,4},{1,3},{4,8},{5,1},{8,12},{9,5},{12,14},{13,9},{14,10},{15,13... | collective-permute-start | bytes 1572872 | tf_op jit(solution)/shard_map/ppermute | solution.py:324
  152.5 21.1 %collective-permute-start.21 = (bf16[64,4096]{1,0:T(8,128)(2,1)}, bf16[64,4096]{1,0:T(8,128)(2,1)}, u32[]{:S(2)}, u32[]{:S(2)}) collective-permute-start(bf16[64,4096]{1,0:T(8,128)(2,1)} %add_convert_fusion.2), channel_id=1, source_target_pairs={{0,4},{1,3},{4,8},{5,1},{8,12},{9,5},{12,14},{13,9},{14,10},{15,13... | collective-permute-start | bytes 1572872 | tf_op jit(solution)/shard_map/ppermute | solution.py:367
  174.9 9.2 %collective-permute-start.23 = (bf16[64,4096]{1,0:T(8,128)(2,1)S(1)}, bf16[64,4096]{1,0:T(8,128)(2,1)S(1)}, u32[]{:S(2)}, u32[]{:S(2)}) collective-permute-start(bf16[64,4096]{1,0:T(8,128)(2,1)S(1)} %add_convert_fusion.1), channel_id=1, source_target_pairs={{0,4},{1,3},{4,8},{5,1},{8,12},{9,5},{12,14},{13,9},{14,10},{15,13... | collective-permute-start | bytes 1572872 | tf_op jit(solution)/shard_map/ppermute | solution.py:367
  (26 other events, 113.7 us)

commit v2 on v0

--- a/solution.py
+++ b/solution.py
@@ -1,6 +1,10 @@
+from functools import partial
+
 import jax
 import jax.numpy as jnp
 from jax import lax
+from jax.experimental import pallas as pl
+from jax.experimental.pallas import tpu as pltpu
 from jax.sharding import PartitionSpec as P
 
 adapter_scale = 0.5
@@ -152,6 +156,337 @@
     return result_sum.astype(jnp.bfloat16)
 
 
+f32, bf16 = jnp.float32, jnp.bfloat16
+in_vmem = pl.BlockSpec(memory_space=pltpu.VMEM)
+in_smem = pl.BlockSpec(memory_space=pltpu.SMEM)
+weight_terms, lane_count, sum_parts = 3, 128, 2
+chunk_plan = {0: (1, 2), 1: (3, 7), 2: (4, 5), 4: (6, 0)}
+
+
+def dot(left, right):
+    return jnp.dot(left, right, preferred_element_type=f32)
+
+
+def ring_order(chips):
+    return list(range(0, chips, 2)) + list(range(1, chips, 2))[::-1]
+
+
+def hop_pairs(order, hops):
+    count = len(order)
+    pairs = []
+    for place in range(count):
+        for core, sign in ((0, 1), (1, -1)):
+            pairs.append((2 * order[place] + core, 2 * order[(place + sign * hops) % count] + core))
+    return pairs
+
+
+def chip_at_hop(me, hop, chips):
+    chip, parity = me // 2, me % 2
+    place = jnp.where(chip % 2 == 0, chip // 2, chips - 1 - chip // 2)
+    there = (place + (1 - 2 * parity) * hop + chips) % chips
+    return jnp.where(there < chips // 2, 2 * there, 2 * (chips - 1 - there) + 1)
+
+
+def hop_of_send(group, send, chips):
+    return jnp.where(group == 0, send, chips - send)
+
+
+def pack_kernel(chips, ids, slots, entry, output, gating, hidden, *refs):
+    me, group = ids[0], ids[1]
+    rank, width_rows = entry.shape[1:]
+    gating_rows, hidden_rows = gating.shape[2], hidden.shape[1]
+    outs, scratch = refs[:-1], refs[-1]
+    for send, target in enumerate(outs):
+        out = target if send < len(outs) - 1 else scratch
+        expert = slots[chip_at_hop(me, hop_of_send(group, send, chips), chips)]
+        out[:width_rows, :rank] = entry[expert].T
+        out[:width_rows, rank:] = output[expert].T
+        out[width_rows:, :rank] = gating[expert].T
+        out[width_rows : width_rows + hidden_rows, rank:] = hidden[expert]
+        out[width_rows + hidden_rows :, rank:] = jnp.zeros((gating_rows - hidden_rows, rank), bf16)
+    size = outs[-1].shape[0]
+    outs[-1][...] = scratch[pl.ds(pl.multiple_of(group * size, 16), size)]
+
+
+def extend_kernel(experts, tokens, routes, weights, out):
+    width = tokens.shape[1]
+    out[:, :width] = tokens[...]
+    left = jnp.concatenate(
+        [
+            jnp.sum(jnp.where(routes[...] == expert, weights[...], 0.0), axis=0, keepdims=True)
+            for expert in range(experts)
+        ],
+        axis=0,
+    )
+    terms = []
+    for _ in range(weight_terms):
+        terms.append(left.astype(bf16).astype(f32))
+        left = left - terms[-1]
+    terms.append(jnp.zeros((lane_count - weight_terms * experts, left.shape[1]), f32))
+    out[:, width:] = jnp.concatenate(terms, axis=0).T.astype(bf16)
+
+
+def join_kernel(*refs):
+    begin = 0
+    for source in refs[:-1]:
+        refs[-1][begin : begin + source.shape[0]] = source[...]
+        begin += source.shape[0]
+
+
+def collect_kernel(chips, ids, own, mine, twins, near_pack):
+    me, group = ids[0], ids[1]
+    size = own.shape[0]
+    near_pack[chip_at_hop(me, 0, chips)] = own[...]
+    for source, side in ((mine, group), (twins, 1 - group)):
+        for send in range(1, chips // 2):
+            chip = chip_at_hop(me, -hop_of_send(side, send, chips), chips)
+            near_pack[chip] = source[(send - 1) * size : send * size]
+        chip = chip_at_hop(me, -(chips // 2), chips)
+        half = pl.ds(pl.multiple_of(side * (size // 2), 16), size // 2)
+        near_pack[chip, half] = source[(chips // 2 - 1) * size :]
+
+
+def load_kernel(parts, *refs):
+    sources, targets, ready, done = refs[:2], refs[2:4], refs[4], refs[5]
+    copies = []
+    for index, (source, target) in enumerate(zip(sources, targets)):
+        size = source.shape[1] // parts
+        for part in range(parts):
+            piece = pl.ds(part * size, size)
+            copy = pltpu.make_async_copy(
+                source.at[:, piece], target.at[:, piece], done.at[index * parts + part]
+            )
+            copy.start()
+            copies.append(copy)
+    for copy in copies:
+        copy.wait()
+    ready[...] = jnp.zeros_like(ready)
+
+
+def load_base(gateup, down, parts=4):
+    return pl.pallas_call(
+        partial(load_kernel, parts),
+        out_shape=[pltpu.VMEM(part.shape, part.dtype) for part in (gateup, down)]
+        + [jax.ShapeDtypeStruct((8, lane_count), f32)],
+        in_specs=[pl.BlockSpec(memory_space=pltpu.HBM)] * 2,
+        out_specs=[in_vmem] * 3,
+        scratch_shapes=[pltpu.SemaphoreType.DMA((2 * parts,))],
+        compiler_params=pltpu.CompilerParams(vmem_limit_bytes=16 * 2**20),
+        name="load_base",
+    )(*[pltpu.with_memory_space_constraint(part, pltpu.HBM) for part in (gateup, down)])
+
+
+def chunk_kernel(blocks, chips, ids, slots, *refs):
+    arrived = refs[:blocks]
+    near_gateup, far_gateup, near_down, far_down, near_pack, far_pack = refs[blocks : blocks + 6]
+    outs, (rows, total, hidden) = refs[blocks + 6 : -3], refs[-3:]
+    parts = len(outs) // blocks
+    me = ids[0]
+    parity = me % 2
+    block_rows, width = arrived[0].shape[0], near_gateup.shape[1]
+    half = near_down.shape[1]
+    rank = near_pack.shape[2] // 2
+    width_rows = width // (2 * chips)
+    gating_rows = near_pack.shape[1] - width_rows
+    hidden_rows = gating_rows // 2
+    in_rank = lax.broadcasted_iota(jnp.int32, (blocks * block_rows, 2 * rank), 1) < rank
+
+    def pack(chip, core, begin, count):
+        part = pl.ds(begin, count)
+        return jnp.where(parity == core, near_pack[chip, part], far_pack[chip, part])
+
+    for index in range(blocks):
+        rows[index * block_rows : (index + 1) * block_rows] = arrived[index][:, :width]
+    total[0] = dot(rows[...], near_gateup[0])
+    total[1] = dot(rows[...], far_gateup[0])
+    low = jnp.zeros((blocks * block_rows, 2 * rank), f32)
+    for chip in range(chips):
+        for core in range(2):
+            begin = (2 * chip + core) * width_rows
+            low = low + dot(rows[:, begin : begin + width_rows], pack(chip, core, 0, width_rows))
+    rank_rows = jnp.where(in_rank, low, 0.0).astype(bf16)
+
+    def adapter(first, part, count):
+        pieces = [pack(first + device // 2, device % 2, part, count) for device in range(chips // 2)]
+        return jnp.concatenate(pieces, axis=0)
+
+    low = None
+    for far in range(2):
+        which = parity if far == 0 else 1 - parity
+        gate_rows = adapter(which * (chips // 4), width_rows, gating_rows)
+        up_rows = adapter(chips // 2 + which * (chips // 4), width_rows, gating_rows)
+        gate = total[far, :, :half] + adapter_scale * contracted_rows(rank_rows, gate_rows)
+        up = total[far, :, half:] + adapter_scale * contracted_rows(rank_rows, up_rows)
+        active = (gate / (1.0 + jnp.exp(-gate)) * up).astype(bf16)
+        hidden[:, far * half : (far + 1) * half] = active
+        pieces = [
+            pack(which * (chips // 2) + device // 2, device % 2, width_rows, hidden_rows)
+            for device in range(chips)
+        ]
+        part = dot(active, jnp.concatenate(pieces, axis=0))
+        low = part if low is None else low + part
+    low_rank = jnp.where(in_rank, 0.0, low).astype(bf16)
+
+    scales = []
+    lane = lax.broadcasted_iota(jnp.int32, (block_rows, lane_count), 1)
+    ours = (lane % chips == slots[me // 2]) & (lane < weight_terms * chips)
+    for source in arrived:
+        terms = jnp.where(ours, source[:, width:].astype(f32), 0.0)
+        scales.append(jnp.sum(terms, axis=1, keepdims=True))
+
+    for chip in range(chips):
+        for core in range(2):
+            begin = (2 * chip + core) * width_rows
+            columns = slice(begin, begin + width_rows)
+            result = dot(hidden[:, :half], near_down[0, :, columns])
+            result = result + dot(hidden[:, half:], far_down[0, :, columns])
+            result = result + adapter_scale * contracted_rows(low_rank, pack(chip, core, 0, width_rows))
+            result = result.astype(bf16).astype(f32)
+            for index in range(blocks):
+                own = result[index * block_rows : (index + 1) * block_rows]
+                part, first = divmod(begin, width // parts)
+                out = outs[index * parts + part]
+                out[:, first : first + width_rows] = (scales[index] * own).astype(bf16)
+
+
+def expert_chunk(ids, slots, rows, base, packs, parts):
+    blocks = len(rows)
+    block_rows, width, both = rows[0].shape[0], base[0].shape[1], base[0].shape[2]
+    chips = packs[0].shape[0]
+    total_rows = blocks * block_rows
+    return pl.pallas_call(
+        partial(chunk_kernel, blocks, chips),
+        out_shape=[jax.ShapeDtypeStruct((block_rows, width // parts), bf16)] * (blocks * parts),
+        in_specs=[in_smem] * 2 + [in_vmem] * (blocks + 6),
+        out_specs=[in_vmem] * (blocks * parts),
+        scratch_shapes=[
+            pltpu.VMEM((total_rows, width), bf16),
+            pltpu.VMEM((2, total_rows, both), f32),
+            pltpu.VMEM((total_rows, both), bf16),
+        ],
+        compiler_params=pltpu.CompilerParams(vmem_limit_bytes=16 * 2**20),
+        cost_estimate=pl.CostEstimate(flops=2**16, bytes_accessed=2**16, transcendentals=0),
+        name="expert_chunk",
+    )(ids, slots, *rows, *base, *packs)
+
+
+def dense_per_device(
+    tokens, routes, route_weights, slot_experts, gateup_base, down_base,
+    entry_factor, gating_factor, hidden_factor, output_factor,
+):
+    chips = lax.axis_size("expert") // 2
+    width_rows, rank = entry_factor.shape[1:]
+    gating_rows = gating_factor.shape[1]
+    order = ring_order(chips)
+    size = width_rows + gating_rows
+    me = lax.axis_index("expert").astype(jnp.int32)
+    ids = jnp.stack((me, lax.axis_index("groups").astype(jnp.int32)))
+    devices = 2 * chips
+
+    def keep(array):
+        return pltpu.with_memory_space_constraint(array, pltpu.VMEM)
+
+    def ahead(block):
+        return lax.ppermute(block, "expert", hop_pairs(order, 1))
+
+    def back(block):
+        return lax.ppermute(block, "expert", hop_pairs(order, -1))
+
+    def send_factors(block, send):
+        pairs = hop_pairs(order, send)
+        pairs += [(devices + here, devices + there) for here, there in hop_pairs(order, -send)]
+        return lax.ppermute(block, ("groups", "expert"), pairs)
+
+    sends = chips // 2 + 1
+    shapes = [jax.ShapeDtypeStruct((size, 2 * rank), bf16)] * (sends - 1)
+    shapes.append(jax.ShapeDtypeStruct((size // 2, 2 * rank), bf16))
+    packed = pl.pallas_call(
+        partial(pack_kernel, chips),
+        out_shape=shapes,
+        in_specs=[in_smem] * 2 + [in_vmem] * 4,
+        out_specs=[in_vmem] * sends,
+        scratch_shapes=[pltpu.VMEM((size, 2 * rank), bf16)],
+        name="pack_factors",
+    )(
+        ids, slot_experts,
+        jnp.swapaxes(entry_factor, 1, 2), jnp.swapaxes(output_factor, 1, 2),
+        jnp.swapaxes(gating_factor, 1, 2), hidden_factor,
+    )
+    tokens, packed = lax.optimization_barrier((tokens, packed))
+    tokens = pl.pallas_call(
+        partial(extend_kernel, chips),
+        out_shape=jax.ShapeDtypeStruct((tokens.shape[0], tokens.shape[1] + lane_count), bf16),
+        in_specs=[in_vmem] * 3,
+        out_specs=in_vmem,
+        name="extend_tokens",
+    )(tokens, routes.T, route_weights.T)
+    rows = {0: tokens, 1: ahead(tokens)}
+    got = [send_factors(packed[send], send) for send in range(1, sends)]
+
+    rows[1], got, gateup, down = lax.optimization_barrier((rows[1], got, gateup_base, down_base))
+    mine = pl.pallas_call(
+        join_kernel,
+        out_shape=jax.ShapeDtypeStruct((sum(part.shape[0] for part in got), 2 * rank), bf16),
+        in_specs=[in_vmem] * (sends - 1),
+        out_specs=in_vmem,
+        name="join_factors",
+    )(*got)
+    twins = lax.ppermute(mine, "groups", [(0, 1), (1, 0)])
+    rows[7] = back(tokens)
+    rows[2] = ahead(rows[1])
+    far_gateup = partner(gateup, "expert", 0)
+    near_gateup, near_down, ready = load_base(gateup, down)
+
+    twins, rows[2], rows[7], ready, down = lax.optimization_barrier((twins, rows[2], rows[7], ready, down_base))
+    near_pack = pl.pallas_call(
+        partial(collect_kernel, chips),
+        out_shape=jax.ShapeDtypeStruct((chips, size, 2 * rank), bf16),
+        in_specs=[in_smem] + [in_vmem] * 3,
+        out_specs=in_vmem,
+        name="order_factors",
+    )(ids, packed[0], mine, twins)
+    far_pack = partner(near_pack, "expert", 0)
+    far_down = partner(down, "expert", 0)
+    base = (near_gateup, keep(far_gateup), near_down, keep(far_down))
+    packs = [keep(near_pack), keep(far_pack)]
+    rows[6] = back(rows[7])
+    rows[3] = ahead(rows[2])
+    rows[5] = back(rows[6])
+    rows[4] = ahead(rows[3])
+    terms = {}
+
+    def compute(members, after):
+        blocks = [rows[hop] for hop in members]
+        if after is not None:
+            blocks, after = lax.optimization_barrier((blocks, after))
+        results = expert_chunk(ids, slot_experts, blocks, base, packs, sum_parts)
+        for index, hop in enumerate(members):
+            terms[hop] = list(results[index * sum_parts : (index + 1) * sum_parts])
+        return after
+
+    compute(chunk_plan[0], None)
+    running = terms[1]
+    for hop in range(2, chips + 1):
+        if hop == 2:
+            running[-1] = compute(chunk_plan[1], running[-1])
+        running = [ahead(part) for part in running]
+        if hop in chunk_plan:
+            running[-1] = compute(chunk_plan[hop], running[-1])
+        running = [
+            (part.astype(f32) + term.astype(f32)).astype(bf16)
+            for part, term in zip(running, terms[hop % chips])
+        ]
+    return jnp.concatenate(running, axis=1)
+
+
+def program(*args):
+    routes, entry_factor, tokens = args[1], args[6], args[0]
+    experts, rank = entry_factor.shape[0], entry_factor.shape[2]
+    every = routes.shape[1] == experts and lax.axis_size("expert") == 2 * experts
+    every = every and lax.axis_size("groups") == 2 and experts == 8 and rank == 64 and tokens.shape[0] == rank
+    return (dense_per_device if every else per_device)(*args)
+
+
 def solution(mesh):
     in_specs = (
         P(("groups", "expert"), None),
@@ -167,5 +502,5 @@
     )
     out_specs = P(("groups", "expert"), None)
     return jax.shard_map(
-        per_device, mesh=mesh, in_specs=in_specs, out_specs=out_specs, check_vma=False
-    )
+        program, mesh=mesh, in_specs=in_specs, out_specs=out_specs, check_vma=False
+    )

time: 325 us -> 127 us (0.39)
  the two profiles are of different devices: /device:TPU:13 before, /device:TPU:0 now
where the time goes in v2:
time: 127 us
  waiting for transfers between devices  51.3 us (40%)
  Pallas kernels  40.8 us (32%)
  starting transfers between devices  30.9 us (24%)
  other arithmetic  2.34 us (2%)
  local copies, waits for them, and re-layouts  1.56 us (1%)
    ppermute x18, waiting for transfers between devices, ahead(): return lax.ppermute(block, 'expert', hop_pairs(order, 1))  31.7 us
    pallas_call x4, Pallas kernels, expert_chunk(): pl.pallas_call(partial(chunk_kernel, blocks, chips), out_shape=[jax.Shape...  28.4 us
    ppermute x18, starting transfers between devices, ahead(): return lax.ppermute(block, 'expert', hop_pairs(order, 1))  18.4 us
    ppermute x3, waiting for transfers between devices, back(): return lax.ppermute(block, 'expert', hop_pairs(order, -1))  10.3 us
    ppermute x4, waiting for transfers between devices, send_factors(): return lax.ppermute(block, ('groups', 'expert'), pairs)  9.3 us
    ppermute x4, starting transfers between devices, send_factors(): return lax.ppermute(block, ('groups', 'expert'), pairs)  7.88 us
    pallas_call x1, Pallas kernels, load_base(): pl.pallas_call(partial(load_kernel, parts), out_shape=[pltpu.VMEM(part.sh...  4.34 us
    ppermute x3, starting transfers between devices, back(): return lax.ppermute(block, 'expert', hop_pairs(order, -1))  3.32 us
  transfers between devices with their start and end apart: 29, of which 14 were waited for; matrix products, arithmetic and copies ran while one was open for 1% of the time, Pallas kernels for 29%

profile of v2, /device:TPU:0, one launch (start us, length us, event | category | flops | bytes accessed | tf_op | source)
XLA Modules:
  0.0 127.1 jit_solution(41553279495919711)
XLA Ops:
  0.6 2.2 %pack_factors.1 = (bf16[352,128]{1,0:T(8,128)(2,1)}, bf16[352,128]{1,0:T(8,128)(2,1)}, bf16[352,128]{1,0:T(8,128)(2,1)}, bf16[352,128]{1,0:T(8,128)(2,1)}, bf16[176,128]{1,0:T(8,128)(2,1)}) custom-call(s32[2]{0:T(128)} %pad_add_fusion.ids, s32[8]{0:T(128)} %slots.9, bf16[8,64,256]{2,1,0:T(8,128)(2,1)} %bitcast.7, bf16[8,64,256]{2,1,0:T(8,128)(2,1)} %bitcast.8, ...), custom_call_target="tpu_custom_call" | custom-call | tf_op jit(solution)/shard_map/pack_factors/pallas_call | solution.py:403
  2.8 2.0 %extend_tokens.1.refs_1_ = bf16[64,4224]{1,0:T(8,128)(2,1)} custom-call(bf16[64,4096]{1,0:T(8,128)(2,1)} %tokens, s32[8,64]{1,0:T(8,128)} %bitcast.10, f32[8,64]{1,0:T(8,128)} %bitcast.11), custom_call_target="tpu_custom_call" | custom-call | tf_op jit(solution)/shard_map/extend_tokens/pallas_call | solution.py:416
  4.8 3.0 %collective-permute-start = (bf16[64,4224]{1,0:T(8,128)(2,1)}, bf16[64,4224]{1,0:T(8,128)(2,1)S(1)}, u32[]{:S(2)}, u32[]{:S(2)}) collective-permute-start(bf16[64,4224]{1,0:T(8,128)(2,1)} %extend_tokens.1.refs_1_), channel_id=1, source_target_pairs={{0,4},{1,3},{4,8},{5,1},{8,12},{9,5},{12,14},{13,9},{14,10},{15,13... | collective-permute-start | bytes 1622024 | tf_op jit(solution)/shard_map/ppermute | solution.py:390
  9.4 2.5 %collective-permute-start.2 = (bf16[352,128]{1,0:T(8,128)(2,1)}, bf16[352,128]{1,0:T(8,128)(2,1)S(1)}, u32[]{:S(2)}, u32[]{:S(2)}) collective-permute-start(bf16[352,128]{1,0:T(8,128)(2,1)} %get-tuple-element.61), channel_id=1, source_target_pairs={{0,8},{1,7},{4,12},{5,3},{8,14},{9,1},{12,10},{13,5},{14,6},{15,9}... | collective-permute-start | bytes 270344 | tf_op jit(solution)/shard_map/ppermute | solution.py:398
  12.2 3.5 %collective-permute-start.4 = (bf16[176,128]{1,0:T(8,128)(2,1)}, bf16[176,128]{1,0:T(8,128)(2,1)S(1)}, u32[]{:S(2)}, u32[]{:S(2)}) collective-permute-start(bf16[176,128]{1,0:T(8,128)(2,1)} %get-tuple-element.63), channel_id=1, source_target_pairs={{0,14},{1,15},{4,10},{5,11},{8,6},{9,7},{12,2},{13,3},{14,0},{15,1... | collective-permute-start | bytes 135176 | tf_op jit(solution)/shard_map/ppermute | solution.py:398
  15.7 8.1 %collective-permute-done.4.refs_3_ = bf16[176,128]{1,0:T(8,128)(2,1)S(1)} collective-permute-done((bf16[176,128]{1,0:T(8,128)(2,1)}, bf16[176,128]{1,0:T(8,128)(2,1)S(1)}, u32[]{:S(2)}, u32[]{:S(2)}) %collective-permute-start.4) | collective-permute-done | bytes 45088 | tf_op jit(solution)/shard_map/ppermute | solution.py:398
  25.2 2.0 %collective-permute-start.6 = (bf16[64,4224]{1,0:T(8,128)(2,1)S(1)}, bf16[64,4224]{1,0:T(8,128)(2,1)}, u32[]{:S(2)}, u32[]{:S(2)}) collective-permute-start(bf16[64,4224]{1,0:T(8,128)(2,1)S(1)} %collective-permute-done.refs_0_), channel_id=1, source_target_pairs={{0,4},{1,3},{4,8},{5,1},{8,12},{9,5},{12,14},{13,9},{14,10},{15,13... | collective-permute-start | bytes 1622024 | tf_op jit(solution)/shard_map/ppermute | solution.py:390
  30.2 10.3 %collective-permute-done.7.refs_1_ = bf16[64,4224]{1,0:T(8,128)(2,1)S(1)} collective-permute-done((bf16[64,4224]{1,0:T(8,128)(2,1)}, bf16[64,4224]{1,0:T(8,128)(2,1)S(1)}, u32[]{:S(2)}, u32[]{:S(2)}) %collective-permute-start.7) | collective-permute-done | bytes 540704 | tf_op jit(solution)/shard_map/ppermute | solution.py:393
  42.0 2.0 %order_factors.1.refs_6_ = bf16[8,352,128]{2,1,0:T(8,128)(2,1)} custom-call(s32[2]{0:T(128)} %pad_add_fusion.ids, bf16[352,128]{1,0:T(8,128)(2,1)} %get-tuple-element.75.own, bf16[1232,128]{1,0:T(8,128)(2,1)} %join_factors.1.mine, bf16[1232,128]{1,0:T(8,128)(2,1)} %copy-done.8), custom_call_target="tpu_custom_call" | custom-call | tf_op jit(solution)/shard_map/order_factors/pallas_call | solution.py:441
  46.1 4.3 %load_base.1 = (bf16[1,4096,768]{2,1,0:T(8,128)(2,1)S(1)}, bf16[1,384,4096]{2,1,0:T(8,128)(2,1)S(1)}, f32[8,128]{1,0:T(8,128)}) custom-call(bf16[1,4096,768]{2,1,0:T(8,128)(2,1)} %refs_0_, bf16[1,384,4096]{2,1,0:T(8,128)(2,1)} %refs_1_), custom_call_target="tpu_custom_call" | custom-call | tf_op jit(solution)/shard_map/load_base/pallas_call | solution.py:267
  50.6 7.3 %expert_chunk.4 = (bf16[64,2048]{1,0:T(8,128)(2,1)S(1)}, bf16[64,2048]{1,0:T(8,128)(2,1)S(1)}, bf16[64,2048]{1,0:T(8,128)(2,1)S(1)}, bf16[64,2048]{1,0:T(8,128)(2,1)S(1)}) custom-call(s32[2]{0:T(128)S(1)} %copy-done.6, s32[8]{0:T(128)S(1)} %copy-done.7, bf16[64,4224]{1,0:T(8,128)(2,1)S(1)} %copy-done.3, bf16[64,4224]{1,0:T(8,128)(2,1)} %collective-permute-done.6.refs_1_, ...), custom_call_target="tpu_custom_call" | custom-call | flops 65536 | bytes 65536 | tf_op jit(solution)/shard_map/expert_chunk/pallas_call | solution.py:357
  61.3 7.0 %expert_chunk.5 = (bf16[64,2048]{1,0:T(8,128)(2,1)S(1)}, bf16[64,2048]{1,0:T(8,128)(2,1)S(1)}, bf16[64,2048]{1,0:T(8,128)(2,1)S(1)}, bf16[64,2048]{1,0:T(8,128)(2,1)S(1)}) custom-call(s32[2]{0:T(128)S(1)} %copy-done.6, s32[8]{0:T(128)S(1)} %copy-done.7, bf16[64,4224]{1,0:T(8,128)(2,1)S(1)} %collective-permute-done.13.refs_0_, ...), custom_call_target="tpu_custom_call" | custom-call | flops 65536 | bytes 65536 | tf_op jit(solution)/shard_map/expert_chunk/pallas_call | solution.py:357
  69.8 5.8 %collective-permute-done.15.refs_0_ = bf16[64,4224]{1,0:T(8,128)(2,1)S(1)} collective-permute-done((bf16[64,4224]{1,0:T(8,128)(2,1)S(1)}, bf16[64,4224]{1,0:T(8,128)(2,1)S(1)}, u32[]{:S(2)}, u32[]{:S(2)}) %collective-permute-start.15) | collective-permute-done | bytes 540704 | tf_op jit(solution)/shard_map/ppermute | solution.py:390
  75.6 2.8 %collective-permute-done.18 = bf16[64,2048]{1,0:T(8,128)(2,1)S(1)} collective-permute-done((bf16[64,2048]{1,0:T(8,128)(2,1)S(1)}, bf16[64,2048]{1,0:T(8,128)(2,1)S(1)}, u32[]{:S(2)}, u32[]{:S(2)}) %collective-permute-start.18) | collective-permute-done | bytes 262176 | tf_op jit(solution)/shard_map/ppermute | solution.py:390
  79.5 7.0 %expert_chunk.6 = (bf16[64,2048]{1,0:T(8,128)(2,1)S(1)}, bf16[64,2048]{1,0:T(8,128)(2,1)S(1)}, bf16[64,2048]{1,0:T(8,128)(2,1)S(1)}, bf16[64,2048]{1,0:T(8,128)(2,1)S(1)}) custom-call(s32[2]{0:T(128)S(1)} %copy-done.6, s32[8]{0:T(128)S(1)} %copy-done.7, bf16[64,4224]{1,0:T(8,128)(2,1)S(1)} %collective-permute-done.15.refs_0_, ...), custom_call_target="tpu_custom_call" | custom-call | flops 65536 | bytes 65536 | tf_op jit(solution)/shard_map/expert_chunk/pallas_call | solution.py:357
  88.4 4.6 %collective-permute-done.14 = bf16[64,2048]{1,0:T(8,128)(2,1)S(1)} collective-permute-done((bf16[64,2048]{1,0:T(8,128)(2,1)S(1)}, bf16[64,2048]{1,0:T(8,128)(2,1)S(1)}, u32[]{:S(2)}, u32[]{:S(2)}) %collective-permute-start.14) | collective-permute-done | bytes 262176 | tf_op jit(solution)/shard_map/ppermute | solution.py:390
  94.0 1.8 %collective-permute-done.22 = bf16[64,2048]{1,0:T(8,128)(2,1)S(1)} collective-permute-done((bf16[64,2048]{1,0:T(8,128)(2,1)S(1)}, bf16[64,2048]{1,0:T(8,128)(2,1)S(1)}, u32[]{:S(2)}, u32[]{:S(2)}) %collective-permute-start.22) | collective-permute-done | bytes 262176 | tf_op jit(solution)/shard_map/ppermute | solution.py:390
  96.8 7.0 %expert_chunk.7 = (bf16[64,2048]{1,0:T(8,128)(2,1)S(1)}, bf16[64,2048]{1,0:T(8,128)(2,1)S(1)}, bf16[64,2048]{1,0:T(8,128)(2,1)S(1)}, bf16[64,2048]{1,0:T(8,128)(2,1)S(1)}) custom-call(s32[2]{0:T(128)S(1)} %copy-done.6, s32[8]{0:T(128)S(1)} %copy-done.7, bf16[64,4224]{1,0:T(8,128)(2,1)S(1)} %collective-permute-done.16.refs_0_, ...), custom_call_target="tpu_custom_call" | custom-call | flops 65536 | bytes 65536 | tf_op jit(solution)/shard_map/expert_chunk/pallas_call | solution.py:357
  106.6 3.8 %collective-permute-done.20 = bf16[64,2048]{1,0:T(8,128)(2,1)S(1)} collective-permute-done((bf16[64,2048]{1,0:T(8,128)(2,1)S(1)}, bf16[64,2048]{1,0:T(8,128)(2,1)S(1)}, u32[]{:S(2)}, u32[]{:S(2)}) %collective-permute-start.20) | collective-permute-done | bytes 262176 | tf_op jit(solution)/shard_map/ppermute | solution.py:390
  111.3 1.9 %collective-permute-done.26 = bf16[64,2048]{1,0:T(8,128)(2,1)S(1)} collective-permute-done((bf16[64,2048]{1,0:T(8,128)(2,1)S(1)}, bf16[64,2048]{1,0:T(8,128)(2,1)S(1)}, u32[]{:S(2)}, u32[]{:S(2)}) %collective-permute-start.26) | collective-permute-done | bytes 262176 | tf_op jit(solution)/shard_map/ppermute | solution.py:390
  114.1 2.8 %collective-permute-done.23 = bf16[64,2048]{1,0:T(8,128)(2,1)S(1)} collective-permute-done((bf16[64,2048]{1,0:T(8,128)(2,1)S(1)}, bf16[64,2048]{1,0:T(8,128)(2,1)S(1)}, u32[]{:S(2)}, u32[]{:S(2)}) %collective-permute-start.23) | collective-permute-done | bytes 262176 | tf_op jit(solution)/shard_map/ppermute | solution.py:390
  117.8 1.9 %collective-permute-done.27 = bf16[64,2048]{1,0:T(8,128)(2,1)S(1)} collective-permute-done((bf16[64,2048]{1,0:T(8,128)(2,1)S(1)}, bf16[64,2048]{1,0:T(8,128)(2,1)S(1)}, u32[]{:S(2)}, u32[]{:S(2)}) %collective-permute-start.27) | collective-permute-done | bytes 262176 | tf_op jit(solution)/shard_map/ppermute | solution.py:390
  120.6 2.8 %collective-permute-done.24 = bf16[64,2048]{1,0:T(8,128)(2,1)S(1)} collective-permute-done((bf16[64,2048]{1,0:T(8,128)(2,1)S(1)}, bf16[64,2048]{1,0:T(8,128)(2,1)S(1)}, u32[]{:S(2)}, u32[]{:S(2)}) %collective-permute-start.24) | collective-permute-done | bytes 262176 | tf_op jit(solution)/shard_map/ppermute | solution.py:390
  123.5 2.7 %collective-permute-done.28 = bf16[64,2048]{1,0:T(8,128)(2,1)S(1)} collective-permute-done((bf16[64,2048]{1,0:T(8,128)(2,1)S(1)}, bf16[64,2048]{1,0:T(8,128)(2,1)S(1)}, u32[]{:S(2)}, u32[]{:S(2)}) %collective-permute-start.28) | collective-permute-done | bytes 262176 | tf_op jit(solution)/shard_map/ppermute | solution.py:390
  (85 shorter events, 27.2 us)
Async XLA Ops:
  4.8 20.2 %collective-permute-start = (bf16[64,4224]{1,0:T(8,128)(2,1)}, bf16[64,4224]{1,0:T(8,128)(2,1)S(1)}, u32[]{:S(2)}, u32[]{:S(2)}) collective-permute-start(bf16[64,4224]{1,0:T(8,128)(2,1)} %extend_tokens.1.refs_1_), channel_id=1, source_target_pairs={{0,4},{1,3},{4,8},{5,1},{8,12},{9,5},{12,14},{13,9},{14,10},{15,13... | collective-permute-start | bytes 1622024 | tf_op jit(solution)/shard_map/ppermute | solution.py:390
  7.9 16.0 %collective-permute-start.1 = (bf16[352,128]{1,0:T(8,128)(2,1)}, bf16[352,128]{1,0:T(8,128)(2,1)S(1)}, u32[]{:S(2)}, u32[]{:S(2)}) collective-permute-start(bf16[352,128]{1,0:T(8,128)(2,1)} %get-tuple-element.60), channel_id=1, source_target_pairs={{0,4},{1,3},{4,8},{5,1},{8,12},{9,5},{12,14},{13,9},{14,10},{15,13... | collective-permute-start | bytes 270344 | tf_op jit(solution)/shard_map/ppermute | solution.py:398
  9.4 14.4 %collective-permute-start.2 = (bf16[352,128]{1,0:T(8,128)(2,1)}, bf16[352,128]{1,0:T(8,128)(2,1)S(1)}, u32[]{:S(2)}, u32[]{:S(2)}) collective-permute-start(bf16[352,128]{1,0:T(8,128)(2,1)} %get-tuple-element.61), channel_id=1, source_target_pairs={{0,8},{1,7},{4,12},{5,3},{8,14},{9,1},{12,10},{13,5},{14,6},{15,9}... | collective-permute-start | bytes 270344 | tf_op jit(solution)/shard_map/ppermute | solution.py:398
  12.0 13.1 %collective-permute-start.3 = (bf16[352,128]{1,0:T(8,128)(2,1)}, bf16[352,128]{1,0:T(8,128)(2,1)S(1)}, u32[]{:S(2)}, u32[]{:S(2)}) collective-permute-start(bf16[352,128]{1,0:T(8,128)(2,1)} %get-tuple-element.62), channel_id=1, source_target_pairs={{0,12},{1,11},{4,14},{5,7},{8,10},{9,3},{12,6},{13,1},{14,2},{15,5... | collective-permute-start | bytes 270344 | tf_op jit(solution)/shard_map/ppermute | solution.py:398
  12.2 11.6 %collective-permute-start.4 = (bf16[176,128]{1,0:T(8,128)(2,1)}, bf16[176,128]{1,0:T(8,128)(2,1)S(1)}, u32[]{:S(2)}, u32[]{:S(2)}) collective-permute-start(bf16[176,128]{1,0:T(8,128)(2,1)} %get-tuple-element.63), channel_id=1, source_target_pairs={{0,14},{1,15},{4,10},{5,11},{8,6},{9,7},{12,2},{13,3},{14,0},{15,1... | collective-permute-start | bytes 135176 | tf_op jit(solution)/shard_map/ppermute | solution.py:398
  25.1 25.4 %collective-permute-start.8 = (bf16[1,4096,768]{2,1,0:T(8,128)(2,1)}, bf16[1,4096,768]{2,1,0:T(8,128)(2,1)}, u32[]{:S(2)}, u32[]{:S(2)}) collective-permute-start(bf16[1,4096,768]{2,1,0:T(8,128)(2,1)} %refs_0_), channel_id=1, source_target_pairs={{0,1},{1,0},{2,3},{3,2},{4,5},{5,4},{6,7},{7,6},{8,9},{9,8},{10,11... | collective-permute-start | bytes 18874376 | tf_op jit(solution)/shard_map/ppermute | solution.py:20
  25.1 15.3 %collective-permute-start.7 = (bf16[64,4224]{1,0:T(8,128)(2,1)}, bf16[64,4224]{1,0:T(8,128)(2,1)S(1)}, u32[]{:S(2)}, u32[]{:S(2)}) collective-permute-start(bf16[64,4224]{1,0:T(8,128)(2,1)} %extend_tokens.1.refs_1_), channel_id=1, source_target_pairs={{0,2},{1,5},{4,0},{5,9},{8,4},{9,13},{12,8},{13,15},{14,12},{15,11... | collective-permute-start | bytes 1622024 | tf_op jit(solution)/shard_map/ppermute | solution.py:393
  25.2 16.1 %collective-permute-start.6 = (bf16[64,4224]{1,0:T(8,128)(2,1)S(1)}, bf16[64,4224]{1,0:T(8,128)(2,1)}, u32[]{:S(2)}, u32[]{:S(2)}) collective-permute-start(bf16[64,4224]{1,0:T(8,128)(2,1)S(1)} %collective-permute-done.refs_0_), channel_id=1, source_target_pairs={{0,4},{1,3},{4,8},{5,1},{8,12},{9,5},{12,14},{13,9},{14,10},{15,13... | collective-permute-start | bytes 1622024 | tf_op jit(solution)/shard_map/ppermute | solution.py:390
  29.0 11.5 %collective-permute-start.5 = (bf16[1232,128]{1,0:T(8,128)(2,1)}, bf16[1232,128]{1,0:T(8,128)(2,1)S(1)}, u32[]{:S(2)}, u32[]{:S(2)}) collective-permute-start(bf16[1232,128]{1,0:T(8,128)(2,1)} %join_factors.1.mine), channel_id=1, source_target_pairs={{0,16},{16,0},{1,17},{17,1},{2,18},{18,2},{3,19},{19,3},{4,20},{20... | collective-permute-start | bytes 946184 | tf_op jit(solution)/shard_map/ppermute | solution.py:434
  41.3 9.2 %collective-permute-start.9 = (bf16[1,384,4096]{2,1,0:T(8,128)(2,1)}, bf16[1,384,4096]{2,1,0:T(8,128)(2,1)S(1)}, u32[]{:S(2)}, u32[]{:S(2)}) collective-permute-start(bf16[1,384,4096]{2,1,0:T(8,128)(2,1)} %refs_1_), channel_id=1, source_target_pairs={{0,1},{1,0},{2,3},{3,2},{4,5},{5,4},{6,7},{7,6},{8,9},{9,8},{10,11... | collective-permute-start | bytes 9437192 | tf_op jit(solution)/shard_map/ppermute | solution.py:20
  44.0 6.4 %collective-permute-start.10 = (bf16[8,352,128]{2,1,0:T(8,128)(2,1)}, bf16[8,352,128]{2,1,0:T(8,128)(2,1)S(1)}, u32[]{:S(2)}, u32[]{:S(2)}) collective-permute-start(bf16[8,352,128]{2,1,0:T(8,128)(2,1)} %order_factors.1.refs_6_), channel_id=1, source_target_pairs={{0,1},{1,0},{2,3},{3,2},{4,5},{5,4},{6,7},{7,6},{8,9},{9,8},{10,11... | collective-permute-start | bytes 2162696 | tf_op jit(solution)/shard_map/ppermute | solution.py:20
  44.1 14.9 %collective-permute-start.13 = (bf16[64,4224]{1,0:T(8,128)(2,1)}, bf16[64,4224]{1,0:T(8,128)(2,1)S(1)}, u32[]{:S(2)}, u32[]{:S(2)}) collective-permute-start(bf16[64,4224]{1,0:T(8,128)(2,1)} %collective-permute-done.6.refs_1_), channel_id=1, source_target_pairs={{0,4},{1,3},{4,8},{5,1},{8,12},{9,5},{12,14},{13,9},{14,10},{15,13... | collective-permute-start | bytes 1622024 | tf_op jit(solution)/shard_map/ppermute | solution.py:390
  44.6 14.7 %collective-permute-start.16 = (bf16[64,4224]{1,0:T(8,128)(2,1)}, bf16[64,4224]{1,0:T(8,128)(2,1)S(1)}, u32[]{:S(2)}, u32[]{:S(2)}) collective-permute-start(bf16[64,4224]{1,0:T(8,128)(2,1)} %copy-done.4), channel_id=1, source_target_pairs={{0,2},{1,5},{4,0},{5,9},{8,4},{9,13},{12,8},{13,15},{14,12},{15,11... | collective-permute-start | bytes 1622024 | tf_op jit(solution)/shard_map/ppermute | solution.py:393
  57.9 10.5 %collective-permute-start.11 = (bf16[64,2048]{1,0:T(8,128)(2,1)S(1)}, bf16[64,2048]{1,0:T(8,128)(2,1)S(1)}, u32[]{:S(2)}, u32[]{:S(2)}) collective-permute-start(bf16[64,2048]{1,0:T(8,128)(2,1)S(1)} %get-tuple-element.77), channel_id=1, source_target_pairs={{0,4},{1,3},{4,8},{5,1},{8,12},{9,5},{12,14},{13,9},{14,10},{15,13... | collective-permute-start | bytes 786440 | tf_op jit(solution)/shard_map/ppermute | solution.py:390
  59.0 16.7 %collective-permute-start.15 = (bf16[64,4224]{1,0:T(8,128)(2,1)S(1)}, bf16[64,4224]{1,0:T(8,128)(2,1)S(1)}, u32[]{:S(2)}, u32[]{:S(2)}) collective-permute-start(bf16[64,4224]{1,0:T(8,128)(2,1)S(1)} %collective-permute-done.13.refs_0_), channel_id=1, source_target_pairs={{0,4},{1,3},{4,8},{5,1},{8,12},{9,5},{12,14},{13,9},{14,10},{15,13... | collective-permute-start | bytes 1622024 | tf_op jit(solution)/shard_map/ppermute | solution.py:390
  59.3 16.3 %collective-permute-start.17 = (bf16[64,4224]{1,0:T(8,128)(2,1)S(1)}, bf16[64,4224]{1,0:T(8,128)(2,1)S(1)}, u32[]{:S(2)}, u32[]{:S(2)}) collective-permute-start(bf16[64,4224]{1,0:T(8,128)(2,1)S(1)} %collective-permute-done.16.refs_0_), channel_id=1, source_target_pairs={{0,2},{1,5},{4,0},{5,9},{8,4},{9,13},{12,8},{13,15},{14,12},{15,11... | collective-permute-start | bytes 1622024 | tf_op jit(solution)/shard_map/ppermute | solution.py:393
  61.0 17.4 %collective-permute-start.18 = (bf16[64,2048]{1,0:T(8,128)(2,1)S(1)}, bf16[64,2048]{1,0:T(8,128)(2,1)S(1)}, u32[]{:S(2)}, u32[]{:S(2)}) collective-permute-start(bf16[64,2048]{1,0:T(8,128)(2,1)S(1)} %get-tuple-element.84), channel_id=1, source_target_pairs={{0,4},{1,3},{4,8},{5,1},{8,12},{9,5},{12,14},{13,9},{14,10},{15,13... | collective-permute-start | bytes 786440 | tf_op jit(solution)/shard_map/ppermute | solution.py:390
  68.4 18.1 %collective-permute-start.12 = (bf16[64,2048]{1,0:T(8,128)(2,1)S(1)}, bf16[64,2048]{1,0:T(8,128)(2,1)S(1)}, u32[]{:S(2)}, u32[]{:S(2)}) collective-permute-start(bf16[64,2048]{1,0:T(8,128)(2,1)S(1)} %add_convert_fusion.13), channel_id=1, source_target_pairs={{0,4},{1,3},{4,8},{5,1},{8,12},{9,5},{12,14},{13,9},{14,10},{15,13... | collective-permute-start | bytes 786440 | tf_op jit(solution)/shard_map/ppermute | solution.py:390
  78.5 9.0 %collective-permute-start.21 = (bf16[64,2048]{1,0:T(8,128)(2,1)S(1)}, bf16[64,2048]{1,0:T(8,128)(2,1)S(1)}, u32[]{:S(2)}, u32[]{:S(2)}) collective-permute-start(bf16[64,2048]{1,0:T(8,128)(2,1)S(1)} %add_convert_fusion.9), channel_id=1, source_target_pairs={{0,4},{1,3},{4,8},{5,1},{8,12},{9,5},{12,14},{13,9},{14,10},{15,13... | collective-permute-start | bytes 786440 | tf_op jit(solution)/shard_map/ppermute | solution.py:390
  86.6 6.4 %collective-permute-start.14 = (bf16[64,2048]{1,0:T(8,128)(2,1)S(1)}, bf16[64,2048]{1,0:T(8,128)(2,1)S(1)}, u32[]{:S(2)}, u32[]{:S(2)}) collective-permute-start(bf16[64,2048]{1,0:T(8,128)(2,1)S(1)} %add_convert_fusion.12), channel_id=1, source_target_pairs={{0,4},{1,3},{4,8},{5,1},{8,12},{9,5},{12,14},{13,9},{14,10},{15,13... | collective-permute-start | bytes 786440 | tf_op jit(solution)/shard_map/ppermute | solution.py:390
  87.6 8.2 %collective-permute-start.22 = (bf16[64,2048]{1,0:T(8,128)(2,1)S(1)}, bf16[64,2048]{1,0:T(8,128)(2,1)S(1)}, u32[]{:S(2)}, u32[]{:S(2)}) collective-permute-start(bf16[64,2048]{1,0:T(8,128)(2,1)S(1)} %add_convert_fusion.8), channel_id=1, source_target_pairs={{0,4},{1,3},{4,8},{5,1},{8,12},{9,5},{12,14},{13,9},{14,10},{15,13... | collective-permute-start | bytes 786440 | tf_op jit(solution)/shard_map/ppermute | solution.py:390
  93.1 10.8 %collective-permute-start.19 = (bf16[64,2048]{1,0:T(8,128)(2,1)S(1)}, bf16[64,2048]{1,0:T(8,128)(2,1)S(1)}, u32[]{:S(2)}, u32[]{:S(2)}) collective-permute-start(bf16[64,2048]{1,0:T(8,128)(2,1)S(1)} %add_convert_fusion.11), channel_id=1, source_target_pairs={{0,4},{1,3},{4,8},{5,1},{8,12},{9,5},{12,14},{13,9},{14,10},{15,13... | collective-permute-start | bytes 786440 | tf_op jit(solution)/shard_map/ppermute | solution.py:390
  95.9 8.9 %collective-permute-start.25 = (bf16[64,2048]{1,0:T(8,128)(2,1)S(1)}, bf16[64,2048]{1,0:T(8,128)(2,1)S(1)}, u32[]{:S(2)}, u32[]{:S(2)}) collective-permute-start(bf16[64,2048]{1,0:T(8,128)(2,1)S(1)} %add_convert_fusion.4), channel_id=1, source_target_pairs={{0,4},{1,3},{4,8},{5,1},{8,12},{9,5},{12,14},{13,9},{14,10},{15,13... | collective-permute-start | bytes 786440 | tf_op jit(solution)/shard_map/ppermute | solution.py:390
  104.8 8.4 %collective-permute-start.26 = (bf16[64,2048]{1,0:T(8,128)(2,1)S(1)}, bf16[64,2048]{1,0:T(8,128)(2,1)S(1)}, u32[]{:S(2)}, u32[]{:S(2)}) collective-permute-start(bf16[64,2048]{1,0:T(8,128)(2,1)S(1)} %add_convert_fusion.3), channel_id=1, source_target_pairs={{0,4},{1,3},{4,8},{5,1},{8,12},{9,5},{12,14},{13,9},{14,10},{15,13... | collective-permute-start | bytes 786440 | tf_op jit(solution)/shard_map/ppermute | solution.py:390
  (18 other events, 198.9 us)

commit v3 on v2

--- a/solution.py
+++ b/solution.py
@@ -160,7 +160,9 @@
 in_vmem = pl.BlockSpec(memory_space=pltpu.VMEM)
 in_smem = pl.BlockSpec(memory_space=pltpu.SMEM)
 weight_terms, lane_count, sum_parts = 3, 128, 2
-chunk_plan = {0: (1, 2), 1: (3, 7), 2: (4, 5), 4: (6, 0)}
+small_cost = pl.CostEstimate(flops=2**16, bytes_accessed=2**16, transcendentals=0)
+chunk_plan = ((1, 2), (3, 7))
+begin_plan, end_plan = {2: (4, 5), 4: (6, 0)}, {3: (4, 5), 5: (6, 0)}
 
 
 def dot(left, right):
@@ -191,8 +193,9 @@
     return jnp.where(group == 0, send, chips - send)
 
 
-def pack_kernel(chips, ids, slots, entry, output, gating, hidden, *refs):
-    me, group = ids[0], ids[1]
+def pack_kernel(chips, slots, tokens, routes, weights, entry, output, gating, hidden, extended, *refs):
+    me, group = lax.axis_index("expert"), lax.axis_index("groups")
+    extend(chips, tokens, routes, weights, extended)
     rank, width_rows = entry.shape[1:]
     gating_rows, hidden_rows = gating.shape[2], hidden.shape[1]
     outs, scratch = refs[:-1], refs[-1]
@@ -208,7 +211,7 @@
     outs[-1][...] = scratch[pl.ds(pl.multiple_of(group * size, 16), size)]
 
 
-def extend_kernel(experts, tokens, routes, weights, out):
+def extend(experts, tokens, routes, weights, out):
     width = tokens.shape[1]
     out[:, :width] = tokens[...]
     left = jnp.concatenate(
@@ -233,8 +236,9 @@
         begin += source.shape[0]
 
 
-def collect_kernel(chips, ids, own, mine, twins, near_pack):
-    me, group = ids[0], ids[1]
+def collect_kernel(chips, own, mine, twins, loaded, near_pack):
+    del loaded
+    me, group = lax.axis_index("expert"), lax.axis_index("groups")
     size = own.shape[0]
     near_pack[chip_at_hop(me, 0, chips)] = own[...]
     for source, side in ((mine, group), (twins, 1 - group)):
@@ -271,19 +275,45 @@
         in_specs=[pl.BlockSpec(memory_space=pltpu.HBM)] * 2,
         out_specs=[in_vmem] * 3,
         scratch_shapes=[pltpu.SemaphoreType.DMA((2 * parts,))],
-        compiler_params=pltpu.CompilerParams(vmem_limit_bytes=16 * 2**20),
+        compiler_params=pltpu.CompilerParams(vmem_limit_bytes=2**20),
+        cost_estimate=small_cost,
         name="load_base",
     )(*[pltpu.with_memory_space_constraint(part, pltpu.HBM) for part in (gateup, down)])
 
 
-def chunk_kernel(blocks, chips, ids, slots, *refs):
+def base_kernel(*refs):
+    near_gateup, far_gateup, total, rows = refs[-4:]
+    arrived = refs[:-4]
+    block_rows, width = arrived[0].shape[0], rows.shape[1]
+    for index, source in enumerate(arrived):
+        rows[index * block_rows : (index + 1) * block_rows] = source[:, :width]
+    total[0] = dot(rows[...], near_gateup[0])
+    total[1] = dot(rows[...], far_gateup[0])
+
+
+def base_chunk(rows, near_gateup, far_gateup):
+    blocks, block_rows = len(rows), rows[0].shape[0]
+    width, both = near_gateup.shape[1:]
+    return pl.pallas_call(
+        base_kernel,
+        out_shape=pltpu.VMEM((2, blocks * block_rows, both), f32),
+        in_specs=[in_vmem] * (blocks + 2),
+        out_specs=in_vmem,
+        scratch_shapes=[pltpu.VMEM((blocks * block_rows, width), bf16)],
+        compiler_params=pltpu.CompilerParams(vmem_limit_bytes=8 * 2**20),
+        cost_estimate=small_cost,
+        name="base_chunk",
+    )(*rows, near_gateup, far_gateup)
+
+
+def rest_kernel(blocks, chips, slots, *refs):
+    me = lax.axis_index("expert")
     arrived = refs[:blocks]
-    near_gateup, far_gateup, near_down, far_down, near_pack, far_pack = refs[blocks : blocks + 6]
-    outs, (rows, total, hidden) = refs[blocks + 6 : -3], refs[-3:]
+    total, near_down, far_down, near_pack, far_pack = refs[blocks : blocks + 5]
+    outs, (rows, hidden) = refs[blocks + 5 : -2], refs[-2:]
     parts = len(outs) // blocks
-    me = ids[0]
     parity = me % 2
-    block_rows, width = arrived[0].shape[0], near_gateup.shape[1]
+    block_rows, width = arrived[0].shape[0], rows.shape[1]
     half = near_down.shape[1]
     rank = near_pack.shape[2] // 2
     width_rows = width // (2 * chips)
@@ -297,8 +327,6 @@
 
     for index in range(blocks):
         rows[index * block_rows : (index + 1) * block_rows] = arrived[index][:, :width]
-    total[0] = dot(rows[...], near_gateup[0])
-    total[1] = dot(rows[...], far_gateup[0])
     low = jnp.zeros((blocks * block_rows, 2 * rank), f32)
     for chip in range(chips):
         for core in range(2):
@@ -349,25 +377,23 @@
                 out[:, first : first + width_rows] = (scales[index] * own).astype(bf16)
 
 
-def expert_chunk(ids, slots, rows, base, packs, parts):
-    blocks = len(rows)
-    block_rows, width, both = rows[0].shape[0], base[0].shape[1], base[0].shape[2]
+def rest_chunk(slots, rows, total, near_down, far_down, packs, parts):
+    blocks, block_rows = len(rows), rows[0].shape[0]
+    width, both = near_down.shape[2], 2 * near_down.shape[1]
     chips = packs[0].shape[0]
-    total_rows = blocks * block_rows
     return pl.pallas_call(
-        partial(chunk_kernel, blocks, chips),
+        partial(rest_kernel, blocks, chips),
         out_shape=[jax.ShapeDtypeStruct((block_rows, width // parts), bf16)] * (blocks * parts),
-        in_specs=[in_smem] * 2 + [in_vmem] * (blocks + 6),
+        in_specs=[in_smem] + [in_vmem] * (blocks + 5),
         out_specs=[in_vmem] * (blocks * parts),
         scratch_shapes=[
-            pltpu.VMEM((total_rows, width), bf16),
-            pltpu.VMEM((2, total_rows, both), f32),
-            pltpu.VMEM((total_rows, both), bf16),
+            pltpu.VMEM((blocks * block_rows, width), bf16),
+            pltpu.VMEM((blocks * block_rows, both), bf16),
         ],
-        compiler_params=pltpu.CompilerParams(vmem_limit_bytes=16 * 2**20),
-        cost_estimate=pl.CostEstimate(flops=2**16, bytes_accessed=2**16, transcendentals=0),
-        name="expert_chunk",
-    )(ids, slots, *rows, *base, *packs)
+        compiler_params=pltpu.CompilerParams(vmem_limit_bytes=8 * 2**20),
+        cost_estimate=small_cost,
+        name="rest_chunk",
+    )(slots, *rows, total, near_down, far_down, *packs)
 
 
 def dense_per_device(
@@ -379,8 +405,6 @@
     gating_rows = gating_factor.shape[1]
     order = ring_order(chips)
     size = width_rows + gating_rows
-    me = lax.axis_index("expert").astype(jnp.int32)
-    ids = jnp.stack((me, lax.axis_index("groups").astype(jnp.int32)))
     devices = 2 * chips
 
     def keep(array):
@@ -400,26 +424,20 @@
     sends = chips // 2 + 1
     shapes = [jax.ShapeDtypeStruct((size, 2 * rank), bf16)] * (sends - 1)
     shapes.append(jax.ShapeDtypeStruct((size // 2, 2 * rank), bf16))
-    packed = pl.pallas_call(
+    extended = jax.ShapeDtypeStruct((tokens.shape[0], tokens.shape[1] + lane_count), bf16)
+    tokens, *packed = pl.pallas_call(
         partial(pack_kernel, chips),
-        out_shape=shapes,
-        in_specs=[in_smem] * 2 + [in_vmem] * 4,
-        out_specs=[in_vmem] * sends,
+        out_shape=[extended] + shapes,
+        in_specs=[in_smem] + [in_vmem] * 7,
+        out_specs=[in_vmem] * (sends + 1),
         scratch_shapes=[pltpu.VMEM((size, 2 * rank), bf16)],
+        cost_estimate=small_cost,
         name="pack_factors",
     )(
-        ids, slot_experts,
+        slot_experts, tokens, routes.T, route_weights.T,
         jnp.swapaxes(entry_factor, 1, 2), jnp.swapaxes(output_factor, 1, 2),
         jnp.swapaxes(gating_factor, 1, 2), hidden_factor,
     )
-    tokens, packed = lax.optimization_barrier((tokens, packed))
-    tokens = pl.pallas_call(
-        partial(extend_kernel, chips),
-        out_shape=jax.ShapeDtypeStruct((tokens.shape[0], tokens.shape[1] + lane_count), bf16),
-        in_specs=[in_vmem] * 3,
-        out_specs=in_vmem,
-        name="extend_tokens",
-    )(tokens, routes.T, route_weights.T)
     rows = {0: tokens, 1: ahead(tokens)}
     got = [send_factors(packed[send], send) for send in range(1, sends)]
 
@@ -429,6 +447,8 @@
         out_shape=jax.ShapeDtypeStruct((sum(part.shape[0] for part in got), 2 * rank), bf16),
         in_specs=[in_vmem] * (sends - 1),
         out_specs=in_vmem,
+        compiler_params=pltpu.CompilerParams(vmem_limit_bytes=8 * 2**20),
+        cost_estimate=small_cost,
         name="join_factors",
     )(*got)
     twins = lax.ppermute(mine, "groups", [(0, 1), (1, 0)])
@@ -441,37 +461,48 @@
     near_pack = pl.pallas_call(
         partial(collect_kernel, chips),
         out_shape=jax.ShapeDtypeStruct((chips, size, 2 * rank), bf16),
-        in_specs=[in_smem] + [in_vmem] * 3,
+        in_specs=[in_vmem] * 4,
         out_specs=in_vmem,
+        compiler_params=pltpu.CompilerParams(vmem_limit_bytes=8 * 2**20),
+        cost_estimate=small_cost,
         name="order_factors",
-    )(ids, packed[0], mine, twins)
+    )(packed[0], mine, twins, ready)
     far_pack = partner(near_pack, "expert", 0)
     far_down = partner(down, "expert", 0)
-    base = (near_gateup, keep(far_gateup), near_down, keep(far_down))
+    gateups, downs = (near_gateup, keep(far_gateup)), (near_down, keep(far_down))
     packs = [keep(near_pack), keep(far_pack)]
     rows[6] = back(rows[7])
     rows[3] = ahead(rows[2])
     rows[5] = back(rows[6])
     rows[4] = ahead(rows[3])
-    terms = {}
-
-    def compute(members, after):
-        blocks = [rows[hop] for hop in members]
-        if after is not None:
-            blocks, after = lax.optimization_barrier((blocks, after))
-        results = expert_chunk(ids, slot_experts, blocks, base, packs, sum_parts)
+    totals, terms = {}, {}
+
+    def tied(blocks, after):
+        return lax.optimization_barrier((blocks, after)) if after is not None else (blocks, after)
+
+    def begin_chunk(members, after=None):
+        blocks, after = tied([rows[hop] for hop in members], after)
+        totals[members] = base_chunk(blocks, *gateups)
+        return after
+
+    def end_chunk(members, after=None):
+        total, after = tied(totals[members], after)
+        results = rest_chunk(slot_experts, [rows[hop] for hop in members], keep(total), *downs, packs, sum_parts)
         for index, hop in enumerate(members):
             terms[hop] = list(results[index * sum_parts : (index + 1) * sum_parts])
         return after
 
-    compute(chunk_plan[0], None)
+    begin_chunk(chunk_plan[0])
+    end_chunk(chunk_plan[0])
     running = terms[1]
+    running[-1] = begin_chunk(chunk_plan[1], running[-1])
+    end_chunk(chunk_plan[1])
     for hop in range(2, chips + 1):
-        if hop == 2:
-            running[-1] = compute(chunk_plan[1], running[-1])
         running = [ahead(part) for part in running]
-        if hop in chunk_plan:
-            running[-1] = compute(chunk_plan[hop], running[-1])
+        if hop in begin_plan:
+            running[-1] = begin_chunk(begin_plan[hop], running[-1])
+        if hop in end_plan:
+            running[-1] = end_chunk(end_plan[hop], running[-1])
         running = [
             (part.astype(f32) + term.astype(f32)).astype(bf16)
             for part, term in zip(running, terms[hop % chips])

time: 127 us -> 112 us (0.88)
  Pallas kernels: 40.8 us -> 26 us
  starting transfers between devices: 30.9 us -> 33.8 us
  local copies, waits for them, and re-layouts: 1.56 us -> 0.02 us
  waiting for transfers between devices: 51.3 us -> 50 us
    pallas_call x6 -> x9, Pallas kernels: 32.7 us -> 22.1 us  [the longest x4 12 us: rest_chunk(): pl.pallas_call(partial(rest_kernel, blocks, chips), out_shape=[jax.ShapeD...]
    ppermute x18, waiting for transfers between devices: 31.7 us -> 27.9 us  [ahead(): return lax.ppermute(block, 'expert', hop_pairs(order, 1))]
    ppermute x18, starting transfers between devices: 18.4 us -> 21.7 us  [ahead(): return lax.ppermute(block, 'expert', hop_pairs(order, 1))]
    ppermute x3, waiting for transfers between devices: 0.01 us -> 2.11 us  [partner(): return lax.ppermute(block, axis, route)]
    pallas_call x1, Pallas kernels: 2.05 us -> 0.08 us  [dense_per_device(): pl.pallas_call(partial(collect_kernel, chips), out_shape=jax.ShapeDtypeSt...]
    pallas_call x1, Pallas kernels: 1.72 us -> 0.02 us  [dense_per_device(): pl.pallas_call(join_kernel, out_shape=jax.ShapeDtypeStruct((sum((part.sha...]
    unnamed x26 -> x8, local copies, waits for them, and re-layouts: 1.56 us -> 0.02 us
  transfers between devices with their start and end apart: 29 -> 29, of which waited for: 14 -> 18; matrix products, arithmetic and copies ran while one was open for 1% -> 1% of each run, Pallas kernels for 29% -> 21%
where the time goes in v3:
time: 112 us
  waiting for transfers between devices  50 us (45%)
  starting transfers between devices  33.8 us (30%)
  Pallas kernels  26 us (23%)
  other arithmetic  1.74 us (2%)
    ppermute x18, waiting for transfers between devices, ahead(): return lax.ppermute(block, 'expert', hop_pairs(order, 1))  27.9 us
    ppermute x18, starting transfers between devices, ahead(): return lax.ppermute(block, 'expert', hop_pairs(order, 1))  21.7 us
    pallas_call x4, Pallas kernels, rest_chunk(): pl.pallas_call(partial(rest_kernel, blocks, chips), out_shape=[jax.ShapeD...  12 us
    ppermute x3, waiting for transfers between devices, back(): return lax.ppermute(block, 'expert', hop_pairs(order, -1))  10.6 us
    ppermute x4, waiting for transfers between devices, send_factors(): return lax.ppermute(block, ('groups', 'expert'), pairs)  9.32 us
    ppermute x4, starting transfers between devices, send_factors(): return lax.ppermute(block, ('groups', 'expert'), pairs)  7.88 us
    pallas_call x4, Pallas kernels, base_chunk(): pl.pallas_call(base_kernel, out_shape=pltpu.VMEM((2, blocks * block_rows,...  7.5 us
    pallas_call x1, Pallas kernels, load_base(): pl.pallas_call(partial(load_kernel, parts), out_shape=[pltpu.VMEM(part.sh...  3.75 us
  transfers between devices with their start and end apart: 29, of which 18 were waited for; matrix products, arithmetic and copies ran while one was open for 1% of the time, Pallas kernels for 21%

profile of v3, /device:TPU:0, one launch (start us, length us, event | category | flops | bytes accessed | tf_op | source)
XLA Modules:
  0.0 111.7 jit_solution(4911354891752673930)
XLA Ops:
  0.0 2.6 %pack_factors.1 = (bf16[64,4224]{1,0:T(8,128)(2,1)}, bf16[352,128]{1,0:T(8,128)(2,1)}, bf16[352,128]{1,0:T(8,128)(2,1)}, bf16[352,128]{1,0:T(8,128)(2,1)}, bf16[...) custom-call(s32[8]{0:T(128)} %slots.9, bf16[64,4096]{1,0:T(8,128)(2,1)} %tokens.1, s32[8,64]{1,0:T(8,128)} %bitcast.8, ...), custom_call_target="tpu_custom_call" | custom-call | flops 65536 | bytes 65536 | tf_op jit(solution)/shard_map/pack_factors/pallas_call | solution.py:428
  2.7 3.1 %collective-permute-start = (bf16[64,4224]{1,0:T(8,128)(2,1)}, bf16[64,4224]{1,0:T(8,128)(2,1)S(1)}, u32[]{:S(2)}, u32[]{:S(2)}) collective-permute-start(bf16[64,4224]{1,0:T(8,128)(2,1)} %get-tuple-element.93.refs_1_), channel_id=1, source_target_pairs={{0,4},{1,3},{4,8},{5,1},{8,12},{9,5},{12,14},{13,9},{14,10},{15,13... | collective-permute-start | bytes 1622024 | tf_op jit(solution)/shard_map/ppermute | solution.py:414
  7.3 2.5 %collective-permute-start.2 = (bf16[352,128]{1,0:T(8,128)(2,1)}, bf16[352,128]{1,0:T(8,128)(2,1)S(1)}, u32[]{:S(2)}, u32[]{:S(2)}) collective-permute-start(bf16[352,128]{1,0:T(8,128)(2,1)} %get-tuple-element.57), channel_id=1, source_target_pairs={{0,8},{1,7},{4,12},{5,3},{8,14},{9,1},{12,10},{13,5},{14,6},{15,9}... | collective-permute-start | bytes 270344 | tf_op jit(solution)/shard_map/ppermute | solution.py:422
  10.1 3.5 %collective-permute-start.4 = (bf16[176,128]{1,0:T(8,128)(2,1)}, bf16[176,128]{1,0:T(8,128)(2,1)S(1)}, u32[]{:S(2)}, u32[]{:S(2)}) collective-permute-start(bf16[176,128]{1,0:T(8,128)(2,1)} %get-tuple-element.59), channel_id=1, source_target_pairs={{0,14},{1,15},{4,10},{5,11},{8,6},{9,7},{12,2},{13,3},{14,0},{15,1... | collective-permute-start | bytes 135176 | tf_op jit(solution)/shard_map/ppermute | solution.py:422
  13.6 8.1 %collective-permute-done.4.refs_3_ = bf16[176,128]{1,0:T(8,128)(2,1)S(1)} collective-permute-done((bf16[176,128]{1,0:T(8,128)(2,1)}, bf16[176,128]{1,0:T(8,128)(2,1)S(1)}, u32[]{:S(2)}, u32[]{:S(2)}) %collective-permute-start.4) | collective-permute-done | bytes 45088 | tf_op jit(solution)/shard_map/ppermute | solution.py:422
  23.0 2.0 %collective-permute-start.6 = (bf16[64,4224]{1,0:T(8,128)(2,1)S(1)}, bf16[64,4224]{1,0:T(8,128)(2,1)S(1)}, u32[]{:S(2)}, u32[]{:S(2)}) collective-permute-start(bf16[64,4224]{1,0:T(8,128)(2,1)S(1)} %collective-permute-done.refs_0_), channel_id=1, source_target_pairs={{0,4},{1,3},{4,8},{5,1},{8,12},{9,5},{12,14},{13,9},{14,10},{15,13... | collective-permute-start | bytes 1622024 | tf_op jit(solution)/shard_map/ppermute | solution.py:414
  26.4 3.7 %load_base.1 = (bf16[1,4096,768]{2,1,0:T(8,128)(2,1)S(1)}, bf16[1,384,4096]{2,1,0:T(8,128)(2,1)S(1)}, f32[8,128]{1,0:T(8,128)S(1)}) custom-call(bf16[1,4096,768]{2,1,0:T(8,128)(2,1)} %refs_0_, bf16[1,384,4096]{2,1,0:T(8,128)(2,1)} %refs_1_), custom_call_target="tpu_custom_call" | custom-call | flops 65536 | bytes 65536 | tf_op jit(solution)/shard_map/load_base/pallas_call | solution.py:271
  30.1 8.0 %collective-permute-done.7.refs_1_ = bf16[64,4224]{1,0:T(8,128)(2,1)S(1)} collective-permute-done((bf16[64,4224]{1,0:T(8,128)(2,1)}, bf16[64,4224]{1,0:T(8,128)(2,1)S(1)}, u32[]{:S(2)}, u32[]{:S(2)}) %collective-permute-start.7) | collective-permute-done | bytes 540704 | tf_op jit(solution)/shard_map/ppermute | solution.py:417
  42.8 2.1 %collective-permute-done.10.refs_6_ = bf16[8,352,128]{2,1,0:T(8,128)(2,1)S(1)} collective-permute-done((bf16[8,352,128]{2,1,0:T(8,128)(2,1)S(1)}, bf16[8,352,128]{2,1,0:T(8,128)(2,1)S(1)}, u32[]{:S(2)}, u32[]{:S(2)}) %collective-permute-start.10) | collective-permute-done | bytes 720928 | tf_op jit(solution)/shard_map/ppermute | solution.py:20
  44.9 3.0 %rest_chunk.4 = (bf16[64,2048]{1,0:T(8,128)(2,1)S(1)}, bf16[64,2048]{1,0:T(8,128)(2,1)S(1)}, bf16[64,2048]{1,0:T(8,128)(2,1)S(1)}, bf16[64,2048]{1,0:T(8,128)(2,1)S(1)}) custom-call(s32[8]{0:T(128)S(1)} %copy-done.2, bf16[64,4224]{1,0:T(8,128)(2,1)S(1)} %collective-permute-done.refs_0_, bf16[64,4224]{1,0:T(8,128)(2,1)S(1)} %collective-permute-done.6.refs_1_, ...), custom_call_target="tpu_custom_call" | custom-call | flops 65536 | bytes 65536 | tf_op jit(solution)/shard_map/rest_chunk/pallas_call | solution.py:384
  48.7 4.5 %collective-permute-done.13.refs_0_ = bf16[64,4224]{1,0:T(8,128)(2,1)S(1)} collective-permute-done((bf16[64,4224]{1,0:T(8,128)(2,1)S(1)}, bf16[64,4224]{1,0:T(8,128)(2,1)S(1)}, u32[]{:S(2)}, u32[]{:S(2)}) %collective-permute-start.13) | collective-permute-done | bytes 540704 | tf_op jit(solution)/shard_map/ppermute | solution.py:414
  55.8 1.9 %base_chunk.5.refs_2_ = f32[2,128,768]{2,1,0:T(8,128)S(1)} custom-call(bf16[64,4224]{1,0:T(8,128)(2,1)S(1)} %collective-permute-done.13.refs_0_, bf16[64,4224]{1,0:T(8,128)(2,1)S(1)} %collective-permute-done.7.refs_1_, bf16[1,4096,768]{2,1,0:T(8,128)(2,1)S(1)} %get-tuple-element.69.refs_2_, bf16[1,4096,768]{2,1,0:T(8,128)(2,1)S(1)} %collective-permute-done.8.refs_3_), custom_call_target="tpu_custom_call" | custom-call | flops 65536 | bytes 65536 | tf_op jit(solution)/shard_map/base_chunk/pallas_call | solution.py:297
  58.8 3.0 %rest_chunk.5 = (bf16[64,2048]{1,0:T(8,128)(2,1)S(1)}, bf16[64,2048]{1,0:T(8,128)(2,1)S(1)}, bf16[64,2048]{1,0:T(8,128)(2,1)S(1)}, bf16[64,2048]{1,0:T(8,128)(2,1)S(1)}) custom-call(s32[8]{0:T(128)S(1)} %copy-done.2, bf16[64,4224]{1,0:T(8,128)(2,1)S(1)} %collective-permute-done.13.refs_0_, bf16[64,4224]{1,0:T(8,128)(2,1)S(1)} %collective-permute-done.7.refs_1_, ...), custom_call_target="tpu_custom_call" | custom-call | flops 65536 | bytes 65536 | tf_op jit(solution)/shard_map/rest_chunk/pallas_call | solution.py:384
  62.7 4.8 %collective-permute-done.15.refs_0_ = bf16[64,4224]{1,0:T(8,128)(2,1)S(1)} collective-permute-done((bf16[64,4224]{1,0:T(8,128)(2,1)S(1)}, bf16[64,4224]{1,0:T(8,128)(2,1)S(1)}, u32[]{:S(2)}, u32[]{:S(2)}) %collective-permute-start.15) | collective-permute-done | bytes 540704 | tf_op jit(solution)/shard_map/ppermute | solution.py:414
  67.6 2.5 %collective-permute-done.17.refs_1_ = bf16[64,4224]{1,0:T(8,128)(2,1)S(1)} collective-permute-done((bf16[64,4224]{1,0:T(8,128)(2,1)S(1)}, bf16[64,4224]{1,0:T(8,128)(2,1)S(1)}, u32[]{:S(2)}, u32[]{:S(2)}) %collective-permute-start.17) | collective-permute-done | bytes 540704 | tf_op jit(solution)/shard_map/ppermute | solution.py:417
  72.3 1.9 %base_chunk.6.refs_2_ = f32[2,128,768]{2,1,0:T(8,128)S(1)} custom-call(bf16[64,4224]{1,0:T(8,128)(2,1)S(1)} %collective-permute-done.15.refs_0_, bf16[64,4224]{1,0:T(8,128)(2,1)S(1)} %collective-permute-done.17.refs_1_, bf16[1,4096,768]{2,1,0:T(8,128)(2,1)S(1)} %get-tuple-element.69.refs_2_, bf16[1,4096,768]{2,1,0:T(8,128)(2,1)S(1)} %collective-permute-done.8.refs_3_), custom_call_target="tpu_custom_call" | custom-call | flops 65536 | bytes 65536 | tf_op jit(solution)/shard_map/base_chunk/pallas_call | solution.py:297
  75.1 1.9 %collective-permute-done.19 = bf16[64,2048]{1,0:T(8,128)(2,1)S(1)} collective-permute-done((bf16[64,2048]{1,0:T(8,128)(2,1)S(1)}, bf16[64,2048]{1,0:T(8,128)(2,1)S(1)}, u32[]{:S(2)}, u32[]{:S(2)}) %collective-permute-start.19) | collective-permute-done | bytes 262176 | tf_op jit(solution)/shard_map/ppermute | solution.py:414
  78.8 3.0 %rest_chunk.6 = (bf16[64,2048]{1,0:T(8,128)(2,1)S(1)}, bf16[64,2048]{1,0:T(8,128)(2,1)S(1)}, bf16[64,2048]{1,0:T(8,128)(2,1)S(1)}, bf16[64,2048]{1,0:T(8,128)(2,1)S(1)}) custom-call(s32[8]{0:T(128)S(1)} %copy-done.2, bf16[64,4224]{1,0:T(8,128)(2,1)S(1)} %collective-permute-done.15.refs_0_, bf16[64,4224]{1,0:T(8,128)(2,1)S(1)} %collective-permute-done.17.refs_1_, ...), custom_call_target="tpu_custom_call" | custom-call | flops 65536 | bytes 65536 | tf_op jit(solution)/shard_map/rest_chunk/pallas_call | solution.py:384
  89.2 1.9 %collective-permute-done.23 = bf16[64,2048]{1,0:T(8,128)(2,1)S(1)} collective-permute-done((bf16[64,2048]{1,0:T(8,128)(2,1)S(1)}, bf16[64,2048]{1,0:T(8,128)(2,1)S(1)}, u32[]{:S(2)}, u32[]{:S(2)}) %collective-permute-start.23) | collective-permute-done | bytes 262176 | tf_op jit(solution)/shard_map/ppermute | solution.py:414
  92.0 3.0 %rest_chunk.7 = (bf16[64,2048]{1,0:T(8,128)(2,1)S(1)}, bf16[64,2048]{1,0:T(8,128)(2,1)S(1)}, bf16[64,2048]{1,0:T(8,128)(2,1)S(1)}, bf16[64,2048]{1,0:T(8,128)(2,1)S(1)}) custom-call(s32[8]{0:T(128)S(1)} %copy-done.2, bf16[64,4224]{1,0:T(8,128)(2,1)S(1)} %collective-permute-done.16.refs_0_, bf16[64,4224]{1,0:T(8,128)(2,1)S(1)} %copy-done, ...), custom_call_target="tpu_custom_call" | custom-call | flops 65536 | bytes 65536 | tf_op jit(solution)/shard_map/rest_chunk/pallas_call | solution.py:384
  98.5 3.0 %collective-permute-done.24 = bf16[64,2048]{1,0:T(8,128)(2,1)S(1)} collective-permute-done((bf16[64,2048]{1,0:T(8,128)(2,1)S(1)}, bf16[64,2048]{1,0:T(8,128)(2,1)S(1)}, u32[]{:S(2)}, u32[]{:S(2)}) %collective-permute-start.24) | collective-permute-done | bytes 262176 | tf_op jit(solution)/shard_map/ppermute | solution.py:414
  102.3 2.0 %collective-permute-done.27 = bf16[64,2048]{1,0:T(8,128)(2,1)S(1)} collective-permute-done((bf16[64,2048]{1,0:T(8,128)(2,1)S(1)}, bf16[64,2048]{1,0:T(8,128)(2,1)S(1)}, u32[]{:S(2)}, u32[]{:S(2)}) %collective-permute-start.27) | collective-permute-done | bytes 262176 | tf_op jit(solution)/shard_map/ppermute | solution.py:414
  105.1 2.9 %collective-permute-done.25 = bf16[64,2048]{1,0:T(8,128)(2,1)S(1)} collective-permute-done((bf16[64,2048]{1,0:T(8,128)(2,1)S(1)}, bf16[64,2048]{1,0:T(8,128)(2,1)S(1)}, u32[]{:S(2)}, u32[]{:S(2)}) %collective-permute-start.25) | collective-permute-done | bytes 262176 | tf_op jit(solution)/shard_map/ppermute | solution.py:414
  108.1 2.7 %collective-permute-done.28 = bf16[64,2048]{1,0:T(8,128)(2,1)S(1)} collective-permute-done((bf16[64,2048]{1,0:T(8,128)(2,1)S(1)}, bf16[64,2048]{1,0:T(8,128)(2,1)S(1)}, u32[]{:S(2)}, u32[]{:S(2)}) %collective-permute-start.28) | collective-permute-done | bytes 262176 | tf_op jit(solution)/shard_map/ppermute | solution.py:414
  (69 shorter events, 33.7 us)
Async XLA Ops:
  2.7 20.3 %collective-permute-start = (bf16[64,4224]{1,0:T(8,128)(2,1)}, bf16[64,4224]{1,0:T(8,128)(2,1)S(1)}, u32[]{:S(2)}, u32[]{:S(2)}) collective-permute-start(bf16[64,4224]{1,0:T(8,128)(2,1)} %get-tuple-element.93.refs_1_), channel_id=1, source_target_pairs={{0,4},{1,3},{4,8},{5,1},{8,12},{9,5},{12,14},{13,9},{14,10},{15,13... | collective-permute-start | bytes 1622024 | tf_op jit(solution)/shard_map/ppermute | solution.py:414
  5.7 16.0 %collective-permute-start.1 = (bf16[352,128]{1,0:T(8,128)(2,1)}, bf16[352,128]{1,0:T(8,128)(2,1)S(1)}, u32[]{:S(2)}, u32[]{:S(2)}) collective-permute-start(bf16[352,128]{1,0:T(8,128)(2,1)} %get-tuple-element.56), channel_id=1, source_target_pairs={{0,4},{1,3},{4,8},{5,1},{8,12},{9,5},{12,14},{13,9},{14,10},{15,13... | collective-permute-start | bytes 270344 | tf_op jit(solution)/shard_map/ppermute | solution.py:422
  7.3 14.4 %collective-permute-start.2 = (bf16[352,128]{1,0:T(8,128)(2,1)}, bf16[352,128]{1,0:T(8,128)(2,1)S(1)}, u32[]{:S(2)}, u32[]{:S(2)}) collective-permute-start(bf16[352,128]{1,0:T(8,128)(2,1)} %get-tuple-element.57), channel_id=1, source_target_pairs={{0,8},{1,7},{4,12},{5,3},{8,14},{9,1},{12,10},{13,5},{14,6},{15,9}... | collective-permute-start | bytes 270344 | tf_op jit(solution)/shard_map/ppermute | solution.py:422
  9.8 13.1 %collective-permute-start.3 = (bf16[352,128]{1,0:T(8,128)(2,1)}, bf16[352,128]{1,0:T(8,128)(2,1)S(1)}, u32[]{:S(2)}, u32[]{:S(2)}) collective-permute-start(bf16[352,128]{1,0:T(8,128)(2,1)} %get-tuple-element.58), channel_id=1, source_target_pairs={{0,12},{1,11},{4,14},{5,7},{8,10},{9,3},{12,6},{13,1},{14,2},{15,5... | collective-permute-start | bytes 270344 | tf_op jit(solution)/shard_map/ppermute | solution.py:422
  10.1 11.6 %collective-permute-start.4 = (bf16[176,128]{1,0:T(8,128)(2,1)}, bf16[176,128]{1,0:T(8,128)(2,1)S(1)}, u32[]{:S(2)}, u32[]{:S(2)}) collective-permute-start(bf16[176,128]{1,0:T(8,128)(2,1)} %get-tuple-element.59), channel_id=1, source_target_pairs={{0,14},{1,15},{4,10},{5,11},{8,6},{9,7},{12,2},{13,3},{14,0},{15,1... | collective-permute-start | bytes 135176 | tf_op jit(solution)/shard_map/ppermute | solution.py:422
  22.9 18.0 %collective-permute-start.8 = (bf16[1,4096,768]{2,1,0:T(8,128)(2,1)}, bf16[1,4096,768]{2,1,0:T(8,128)(2,1)S(1)}, u32[]{:S(2)}, u32[]{:S(2)}) collective-permute-start(bf16[1,4096,768]{2,1,0:T(8,128)(2,1)} %refs_0_), channel_id=1, source_target_pairs={{0,1},{1,0},{2,3},{3,2},{4,5},{5,4},{6,7},{7,6},{8,9},{9,8},{10,11... | collective-permute-start | bytes 18874376 | tf_op jit(solution)/shard_map/ppermute | solution.py:20
  22.9 15.2 %collective-permute-start.7 = (bf16[64,4224]{1,0:T(8,128)(2,1)}, bf16[64,4224]{1,0:T(8,128)(2,1)S(1)}, u32[]{:S(2)}, u32[]{:S(2)}) collective-permute-start(bf16[64,4224]{1,0:T(8,128)(2,1)} %get-tuple-element.93.refs_1_), channel_id=1, source_target_pairs={{0,2},{1,5},{4,0},{5,9},{8,4},{9,13},{12,8},{13,15},{14,12},{15,11... | collective-permute-start | bytes 1622024 | tf_op jit(solution)/shard_map/ppermute | solution.py:417
  23.0 15.2 %collective-permute-start.6 = (bf16[64,4224]{1,0:T(8,128)(2,1)S(1)}, bf16[64,4224]{1,0:T(8,128)(2,1)S(1)}, u32[]{:S(2)}, u32[]{:S(2)}) collective-permute-start(bf16[64,4224]{1,0:T(8,128)(2,1)S(1)} %collective-permute-done.refs_0_), channel_id=1, source_target_pairs={{0,4},{1,3},{4,8},{5,1},{8,12},{9,5},{12,14},{13,9},{14,10},{15,13... | collective-permute-start | bytes 1622024 | tf_op jit(solution)/shard_map/ppermute | solution.py:414
  25.0 13.1 %collective-permute-start.5 = (bf16[1232,128]{1,0:T(8,128)(2,1)S(1)}, bf16[1232,128]{1,0:T(8,128)(2,1)S(1)}, u32[]{:S(2)}, u32[]{:S(2)}) collective-permute-start(bf16[1232,128]{1,0:T(8,128)(2,1)S(1)} %join_factors.1.mine), channel_id=1, source_target_pairs={{0,16},{16,0},{1,17},{17,1},{2,18},{18,2},{3,19},{19,3},{4,20},{20... | collective-permute-start | bytes 946184 | tf_op jit(solution)/shard_map/ppermute | solution.py:454
  38.1 6.8 %collective-permute-start.9 = (bf16[1,384,4096]{2,1,0:T(8,128)(2,1)S(1)}, bf16[1,384,4096]{2,1,0:T(8,128)(2,1)S(1)}, u32[]{:S(2)}, u32[]{:S(2)}) collective-permute-start(bf16[1,384,4096]{2,1,0:T(8,128)(2,1)S(1)} %copy-done.3), channel_id=1, source_target_pairs={{0,1},{1,0},{2,3},{3,2},{4,5},{5,4},{6,7},{7,6},{8,9},{9,8},{10,11... | collective-permute-start | bytes 9437192 | tf_op jit(solution)/shard_map/ppermute | solution.py:20
  38.3 6.6 %collective-permute-start.10 = (bf16[8,352,128]{2,1,0:T(8,128)(2,1)S(1)}, bf16[8,352,128]{2,1,0:T(8,128)(2,1)S(1)}, u32[]{:S(2)}, u32[]{:S(2)}) collective-permute-start(bf16[8,352,128]{2,1,0:T(8,128)(2,1)S(1)} %order_factors.1.refs_5_), channel_id=1, source_target_pairs={{0,1},{1,0},{2,3},{3,2},{4,5},{5,4},{6,7},{7,6},{8,9},{9,8},{10,11... | collective-permute-start | bytes 2162696 | tf_op jit(solution)/shard_map/ppermute | solution.py:20
  38.9 14.3 %collective-permute-start.13 = (bf16[64,4224]{1,0:T(8,128)(2,1)S(1)}, bf16[64,4224]{1,0:T(8,128)(2,1)S(1)}, u32[]{:S(2)}, u32[]{:S(2)}) collective-permute-start(bf16[64,4224]{1,0:T(8,128)(2,1)S(1)} %collective-permute-done.6.refs_1_), channel_id=1, source_target_pairs={{0,4},{1,3},{4,8},{5,1},{8,12},{9,5},{12,14},{13,9},{14,10},{15,13... | collective-permute-start | bytes 1622024 | tf_op jit(solution)/shard_map/ppermute | solution.py:414
  39.6 15.2 %collective-permute-start.16 = (bf16[64,4224]{1,0:T(8,128)(2,1)S(1)}, bf16[64,4224]{1,0:T(8,128)(2,1)S(1)}, u32[]{:S(2)}, u32[]{:S(2)}) collective-permute-start(bf16[64,4224]{1,0:T(8,128)(2,1)S(1)} %collective-permute-done.7.refs_1_), channel_id=1, source_target_pairs={{0,2},{1,5},{4,0},{5,9},{8,4},{9,13},{12,8},{13,15},{14,12},{15,11... | collective-permute-start | bytes 1622024 | tf_op jit(solution)/shard_map/ppermute | solution.py:417
  47.9 14.0 %collective-permute-start.11 = (bf16[64,2048]{1,0:T(8,128)(2,1)S(1)}, bf16[64,2048]{1,0:T(8,128)(2,1)S(1)}, u32[]{:S(2)}, u32[]{:S(2)}) collective-permute-start(bf16[64,2048]{1,0:T(8,128)(2,1)S(1)} %get-tuple-element.75), channel_id=1, source_target_pairs={{0,4},{1,3},{4,8},{5,1},{8,12},{9,5},{12,14},{13,9},{14,10},{15,13... | collective-permute-start | bytes 786440 | tf_op jit(solution)/shard_map/ppermute | solution.py:414
  53.2 14.4 %collective-permute-start.15 = (bf16[64,4224]{1,0:T(8,128)(2,1)S(1)}, bf16[64,4224]{1,0:T(8,128)(2,1)S(1)}, u32[]{:S(2)}, u32[]{:S(2)}) collective-permute-start(bf16[64,4224]{1,0:T(8,128)(2,1)S(1)} %collective-permute-done.13.refs_0_), channel_id=1, source_target_pairs={{0,4},{1,3},{4,8},{5,1},{8,12},{9,5},{12,14},{13,9},{14,10},{15,13... | collective-permute-start | bytes 1622024 | tf_op jit(solution)/shard_map/ppermute | solution.py:414
  54.9 15.2 %collective-permute-start.17 = (bf16[64,4224]{1,0:T(8,128)(2,1)S(1)}, bf16[64,4224]{1,0:T(8,128)(2,1)S(1)}, u32[]{:S(2)}, u32[]{:S(2)}) collective-permute-start(bf16[64,4224]{1,0:T(8,128)(2,1)S(1)} %collective-permute-done.16.refs_0_), channel_id=1, source_target_pairs={{0,2},{1,5},{4,0},{5,9},{8,4},{9,13},{12,8},{13,15},{14,12},{15,11... | collective-permute-start | bytes 1622024 | tf_op jit(solution)/shard_map/ppermute | solution.py:417
  57.7 12.7 %collective-permute-start.18 = (bf16[64,2048]{1,0:T(8,128)(2,1)S(1)}, bf16[64,2048]{1,0:T(8,128)(2,1)S(1)}, u32[]{:S(2)}, u32[]{:S(2)}) collective-permute-start(bf16[64,2048]{1,0:T(8,128)(2,1)S(1)} %get-tuple-element.82), channel_id=1, source_target_pairs={{0,4},{1,3},{4,8},{5,1},{8,12},{9,5},{12,14},{13,9},{14,10},{15,13... | collective-permute-start | bytes 786440 | tf_op jit(solution)/shard_map/ppermute | solution.py:414
  61.9 12.3 %collective-permute-start.12 = (bf16[64,2048]{1,0:T(8,128)(2,1)S(1)}, bf16[64,2048]{1,0:T(8,128)(2,1)S(1)}, u32[]{:S(2)}, u32[]{:S(2)}) collective-permute-start(bf16[64,2048]{1,0:T(8,128)(2,1)S(1)} %add_convert_fusion.13), channel_id=1, source_target_pairs={{0,4},{1,3},{4,8},{5,1},{8,12},{9,5},{12,14},{13,9},{14,10},{15,13... | collective-permute-start | bytes 786440 | tf_op jit(solution)/shard_map/ppermute | solution.py:414
  70.5 6.6 %collective-permute-start.19 = (bf16[64,2048]{1,0:T(8,128)(2,1)S(1)}, bf16[64,2048]{1,0:T(8,128)(2,1)S(1)}, u32[]{:S(2)}, u32[]{:S(2)}) collective-permute-start(bf16[64,2048]{1,0:T(8,128)(2,1)S(1)} %add_convert_fusion.11), channel_id=1, source_target_pairs={{0,4},{1,3},{4,8},{5,1},{8,12},{9,5},{12,14},{13,9},{14,10},{15,13... | collective-permute-start | bytes 786440 | tf_op jit(solution)/shard_map/ppermute | solution.py:414
  74.3 7.5 %collective-permute-start.14 = (bf16[64,2048]{1,0:T(8,128)(2,1)S(1)}, bf16[64,2048]{1,0:T(8,128)(2,1)S(1)}, u32[]{:S(2)}, u32[]{:S(2)}) collective-permute-start(bf16[64,2048]{1,0:T(8,128)(2,1)S(1)} %add_convert_fusion.12), channel_id=1, source_target_pairs={{0,4},{1,3},{4,8},{5,1},{8,12},{9,5},{12,14},{13,9},{14,10},{15,13... | collective-permute-start | bytes 786440 | tf_op jit(solution)/shard_map/ppermute | solution.py:414
  83.6 7.5 %collective-permute-start.23 = (bf16[64,2048]{1,0:T(8,128)(2,1)S(1)}, bf16[64,2048]{1,0:T(8,128)(2,1)S(1)}, u32[]{:S(2)}, u32[]{:S(2)}) collective-permute-start(bf16[64,2048]{1,0:T(8,128)(2,1)S(1)} %add_convert_fusion.7), channel_id=1, source_target_pairs={{0,4},{1,3},{4,8},{5,1},{8,12},{9,5},{12,14},{13,9},{14,10},{15,13... | collective-permute-start | bytes 786440 | tf_op jit(solution)/shard_map/ppermute | solution.py:414
  88.4 6.6 %collective-permute-start.21 = (bf16[64,2048]{1,0:T(8,128)(2,1)S(1)}, bf16[64,2048]{1,0:T(8,128)(2,1)S(1)}, u32[]{:S(2)}, u32[]{:S(2)}) collective-permute-start(bf16[64,2048]{1,0:T(8,128)(2,1)S(1)} %add_convert_fusion.9), channel_id=1, source_target_pairs={{0,4},{1,3},{4,8},{5,1},{8,12},{9,5},{12,14},{13,9},{14,10},{15,13... | collective-permute-start | bytes 786440 | tf_op jit(solution)/shard_map/ppermute | solution.py:414
  91.2 6.4 %collective-permute-start.26 = (bf16[64,2048]{1,0:T(8,128)(2,1)S(1)}, bf16[64,2048]{1,0:T(8,128)(2,1)S(1)}, u32[]{:S(2)}, u32[]{:S(2)}) collective-permute-start(bf16[64,2048]{1,0:T(8,128)(2,1)S(1)} %add_convert_fusion.3), channel_id=1, source_target_pairs={{0,4},{1,3},{4,8},{5,1},{8,12},{9,5},{12,14},{13,9},{14,10},{15,13... | collective-permute-start | bytes 786440 | tf_op jit(solution)/shard_map/ppermute | solution.py:414
  97.7 6.6 %collective-permute-start.27 = (bf16[64,2048]{1,0:T(8,128)(2,1)S(1)}, bf16[64,2048]{1,0:T(8,128)(2,1)S(1)}, u32[]{:S(2)}, u32[]{:S(2)}) collective-permute-start(bf16[64,2048]{1,0:T(8,128)(2,1)S(1)} %add_convert_fusion.2), channel_id=1, source_target_pairs={{0,4},{1,3},{4,8},{5,1},{8,12},{9,5},{12,14},{13,9},{14,10},{15,13... | collective-permute-start | bytes 786440 | tf_op jit(solution)/shard_map/ppermute | solution.py:414
  (9 other events, 118.3 us)
